TPU v7x, 32 devices: a whole 2x2x4 slice. The times are simulated.
32 devices in a mesh: ctx: 4 (over y, core), fsdp: 8 (over z, x).
Axes of the slice: x: 2, y: 2, z: 4, core: 2. Of those that a mesh axis runs over, the one named last changes fastest.
Arguments:
- hidden: bfloat16 [8, 1024, 2048], P('fsdp', 'ctx'), may hold values from -6 to 6
- cotangent: bfloat16 [8, 1024, 2048], P('fsdp', 'ctx'), may hold values from -6 to 6
- seq_lens: int32 [8], P('fsdp'), may hold values from 512 to 1024, as said below
- norm_gain: bfloat16 [2048], P('fsdp'), may hold values from 0.5 to 1.5
- in_weight: bfloat16 [2048, 8512], P('fsdp'), may hold values from -0.125 to 0.125
- conv_weight: bfloat16 [4, 4352], P(None, 'fsdp'), may hold values from -3 to 3
- conv_bias: bfloat16 [4352], P('fsdp'), may hold values from -3 to 3
- dt_bias: bfloat16 [64], P('fsdp'), may hold values from -6 to -4
- a_log: bfloat16 [64], P('fsdp'), may hold values from -3 to 1.59375
- d_skip: bfloat16 [64], P('fsdp'), may hold values from 0.5 to 4
- gate_gain: bfloat16 [4096], P('fsdp'), may hold values from 0.5 to 1.5
- out_weight: bfloat16 [4096, 2048], P('fsdp'), may hold values from -0.09375 to 0.09375
Outputs:
- layer_out: bfloat16 [8, 1024, 2048], P('fsdp', 'ctx')
- hidden_grad: bfloat16 [8, 1024, 2048], P('fsdp', 'ctx')
- norm_gain_grad: float32 [2048], P('fsdp')
- in_weight_grad: float32 [2048, 8512], P('fsdp')
- conv_weight_grad: float32 [4, 4352], P(None, 'fsdp')
- conv_bias_grad: float32 [4352], P('fsdp')
- dt_bias_grad: float32 [64], P('fsdp')
- a_log_grad: float32 [64], P('fsdp')
- d_skip_grad: float32 [64], P('fsdp')
- gate_gain_grad: float32 [4096], P('fsdp')
- out_weight_grad: float32 [4096, 2048], P('fsdp')
Inputs may be any that keep to these rules, and one draw needn't show every extreme that they name: A sequence's first seq_lens tokens are valid, the rest padding; some sequence is full and some holds exactly 512 valid tokens.
All inputs are finite; a program needn't handle non-finite values.
Results may differ from a plain program's by a relative error of at most 0.015.
Values may be sent and summed in bfloat16 or wider, within the bound.
A program may use at most 224 MiB of HBM per device.

v0:
```python
import functools

import jax
import jax.numpy as jnp
from jax import lax
from jax.experimental import pallas as pl
from jax.experimental.pallas import tpu as pltpu
from jax.sharding import PartitionSpec as P

HEAD = 64
STATE = 128
BLOCK = 256
LANES = 128
POINTS = 4
EPS = 1e-05
F32 = jnp.float32
BF16 = jnp.bfloat16


def mm(a, b, contract=((1,), (0,))):
    return lax.dot_general(a, b, (contract, ((), ())), preferred_element_type=F32)


def mm_exact(a, b, contract=((1,), (0,))):
    return lax.dot_general(
        a, b, (contract, ((), ())), precision=lax.Precision.HIGHEST, preferred_element_type=F32
    )


def iota2(shape, axis):
    return lax.broadcasted_iota(jnp.int32, shape, axis)


def levels(lam, step):
    tri = (iota2((BLOCK, BLOCK), 0) >= iota2((BLOCK, BLOCK), 1)).astype(F32)
    level = mm_exact(tri, lam)
    across = level.T
    last = level[BLOCK - 1 : BLOCK, :]
    weight = jnp.exp(level - last) * step
    return level, across, jnp.exp(-last), weight, jnp.exp(-level)


def pair_of(array, first, low_half):
    return jnp.where(low_half, array[:, first : first + 1], array[:, first + 1 : first + 2])


def spread(level, across, head):
    return jnp.exp(-jnp.abs(level[:, head : head + 1] - across[head : head + 1, :]))


def silu_and_slope(v):
    s = jax.nn.sigmoid(v)
    return v * s, s * (1.0 + v * (1.0 - s))


def chosen_heads(me, heads, unit, n_ctx, turned=False):
    here, there = iota2((LANES, LANES), 1), iota2((LANES, LANES), 0)
    if turned:
        here, there = there, here
    head = (here // unit * n_ctx + me) * unit + here % unit
    return jnp.where(jnp.logical_and(there == head, here < heads), 1.0, 0.0).astype(BF16)


def column_valid(length_ref, block):
    at = iota2((BLOCK, 1), 0) + block * BLOCK
    return (at < length_ref[0]).astype(F32)


def forward_kernel(
    heads,
    unit,
    n_ctx,
    length_ref,
    px_ref,
    ps_ref,
    pz_ref,
    up_ref,
    w_o,
    taps_x_ref,
    taps_s_ref,
    gate_gain_ref,
    skip_ref,
    head_ref,
    x_ref,
    b_ref,
    c_ref,
    slope_x_ref,
    slope_s_ref,
    lam_ref,
    step_ref,
    chain_ref,
    kept_ref,
    y_ref,
    dyn_ref,
    stat_ref,
    state,
    before_x,
    before_s,
    v_o,
    load_sem,
):
    block = pl.program_id(0)
    load = pltpu.make_async_copy(w_o, v_o, load_sem)

    @pl.when(block == 0)
    def _():
        load.start()
        state[...] = jnp.zeros_like(state)
        before_x[...] = jnp.zeros_like(before_x)
        before_s[...] = jnp.zeros_like(before_s)

    valid = column_valid(length_ref, block)
    low_half = iota2((1, LANES), 1) < HEAD
    taps = taps_x_ref.shape[0] - 1

    def conv(current, before, weight):
        padded = jnp.concatenate([before, current], axis=0)
        total = weight[taps : taps + 1]
        for k in range(taps):
            first = 8 - (taps - 1) + k
            total = total + weight[k : k + 1] * padded[first : first + BLOCK]
        return silu_and_slope(total)

    shared = ps_ref[...].astype(F32)
    both = shared[:, : 2 * STATE]
    active, slope = conv(both, before_s[...], taps_s_ref[...])
    before_s[...] = both[BLOCK - 8 :]
    slope_s_ref[...] = slope.astype(BF16)
    rows_b, rows_c = active[:, :STATE].astype(BF16), active[:, STATE:].astype(BF16)
    b_ref[...] = rows_b
    c_ref[...] = rows_c
    chosen = chosen_heads(lax.axis_index("ctx"), heads, unit, n_ctx)
    raw = mm(ps_ref[:, 2 * STATE :], chosen)
    raw = raw + head_ref[0:1]
    own = iota2((1, LANES), 1) < heads
    step = jnp.where(own, valid * jax.nn.softplus(raw), 0.0)
    lam = step * head_ref[1:2]
    step_ref[...] = step
    lam_ref[...] = lam
    chain_ref[...] = jnp.where(own, valid * jax.nn.sigmoid(raw), 0.0)

    gram = mm(rows_c, rows_b, ((1,), (1,)))
    level, across, last, weight, fade = levels(lam, step)
    kept_ref[0] = state[...].astype(BF16)
    entering = mm(rows_c, state[...].astype(BF16))
    by_state = rows_b.T
    squares = jnp.zeros((BLOCK, LANES), F32)
    for first in range(0, heads, 2):
        lanes = slice(first * HEAD, (first + 2) * HEAD)
        current = px_ref[:, lanes].astype(F32)
        active, slope = conv(current, before_x[:, lanes], taps_x_ref[:, lanes])
        before_x[:, lanes] = current[BLOCK - 8 :]
        slope_x_ref[:, lanes] = slope.astype(BF16)
        x_low = active.astype(BF16)
        x_ref[:, lanes] = x_low
        x = x_low.astype(F32)
        scaled = x * pair_of(step, first, low_half)
        total = pair_of(fade, first, low_half) * entering[:, lanes] + skip_ref[:, lanes] * x
        for head, keep in ((first, low_half), (first + 1, jnp.logical_not(low_half))):
            mixing = (gram * spread(level, across, head)).astype(BF16)
            total += mm(mixing, jnp.where(keep, scaled, 0.0).astype(BF16))
        y_ref[:, lanes] = total
        update = mm(by_state, (x * pair_of(weight, first, low_half)).astype(BF16))
        state[:, lanes] = state[:, lanes] * pair_of(last, first, low_half) + update
        gated = total * jax.nn.silu(pz_ref[:, lanes].astype(F32))
        squares += gated * gated

    @pl.when(block == 0)
    def _():
        load.wait()

    d_yn = valid * mm(up_ref[0], v_o[...], ((1,), (1,)))
    dyn_ref[...] = d_yn
    gated = y_ref[...] * jax.nn.silu(pz_ref[...].astype(F32))
    terms = gate_gain_ref[...] * d_yn * gated
    square = jnp.sum(squares, axis=1, keepdims=True)
    along = jnp.sum(terms, axis=1, keepdims=True)
    lane = iota2((1, LANES), 1)
    both_sums = jnp.where(lane == 0, square, 0.0) + jnp.where(lane == 1, along, 0.0)
    stat_ref[...] = both_sums.T[0:8]


def scan_forward(unit, n_ctx, length, px, ps, pz, upstream, w_o, taps_x, taps_s, gate_gain, skip, head):
    tokens, width = px.shape
    heads = width // HEAD
    count = tokens // BLOCK
    model = w_o.shape[1]
    by_block = lambda i: (i, 0)
    at_block = lambda size: pl.BlockSpec((BLOCK, size), by_block)
    whole = lambda a: pl.BlockSpec(a.shape, lambda i: (0, 0))
    low = lambda *shape: jax.ShapeDtypeStruct(shape, BF16)
    full = lambda *shape: jax.ShapeDtypeStruct(shape, F32)
    return pl.pallas_call(
        functools.partial(forward_kernel, heads, unit, n_ctx),
        grid=(count,),
        in_specs=[
            pl.BlockSpec(memory_space=pltpu.SMEM),
            at_block(width),
            at_block(ps.shape[1]),
            at_block(width),
            pl.BlockSpec((1, BLOCK, model), lambda i: (i, 0, 0)),
            pl.BlockSpec(memory_space=pl.ANY),
            whole(taps_x),
            whole(taps_s),
            whole(gate_gain),
            whole(skip),
            whole(head),
        ],
        out_specs=[
            at_block(width),
            at_block(STATE),
            at_block(STATE),
            at_block(width),
            at_block(2 * STATE),
            at_block(LANES),
            at_block(LANES),
            at_block(LANES),
            pl.BlockSpec((1, STATE, width), lambda i: (i, 0, 0)),
            at_block(width),
            at_block(width),
            pl.BlockSpec((8, BLOCK), lambda i: (0, i)),
        ],
        out_shape=[
            low(tokens, width),
            low(tokens, STATE),
            low(tokens, STATE),
            low(tokens, width),
            low(tokens, 2 * STATE),
            full(tokens, LANES),
            full(tokens, LANES),
            full(tokens, LANES),
            low(count, STATE, width),
            full(tokens, width),
            full(tokens, width),
            full(8, tokens),
        ],
        scratch_shapes=[
            pltpu.VMEM((STATE, width), F32),
            pltpu.VMEM((8, width), F32),
            pltpu.VMEM((8, 2 * STATE), F32),
            pltpu.VMEM(w_o.shape, BF16),
            pltpu.SemaphoreType.DMA,
        ],
        compiler_params=pltpu.CompilerParams(vmem_limit_bytes=56 * 1024 * 1024),
        cost_estimate=pl.CostEstimate(
            flops=2 * tokens * width * (2 * BLOCK + 2 * STATE + model),
            bytes_accessed=tokens * width * 24,
            transcendentals=tokens * heads * BLOCK,
        ),
        name="scan_forward",
    )(length, px, ps, pz, upstream, w_o, taps_x, taps_s, gate_gain, skip, head)


def head_sums(product, chooser):
    high = product.astype(BF16)
    rest = (product - high.astype(F32)).astype(BF16)
    return mm(high, chooser) + mm(rest, chooser)


MESH = pl.DeviceIdType.MESH
SMALL_ROWS = 32


def ring_place(index, half):
    a, b = index // 2, index % 2
    return a + b * (2 * half - 1 - 2 * a)


def ring_index(place, half):
    b = place // half
    return 2 * (place + b * (2 * half - 1 - 2 * place)) + b


class Ring:
    def __init__(self, n):
        self.n, self.half = n, n // 2
        self.me, self.shard = lax.axis_index("ctx"), lax.axis_index("fsdp")
        self.place = ring_place(self.shard, self.half)

    def at(self, steps):
        return ring_index(lax.rem(self.place + steps + 2 * self.n, self.n), self.half)

    def neighbour(self, way):
        return (self.me, self.at(1 if way == 0 else -1))


def remote(source, target, send, recv, device):
    return pltpu.make_async_remote_copy(
        src_ref=source,
        dst_ref=target,
        send_sem=send,
        recv_sem=recv,
        device_id=device,
        device_id_type=MESH,
    )


def greet(device):
    pl.semaphore_signal(pltpu.get_barrier_semaphore(), inc=1, device_id=device, device_id_type=MESH)


class Around:
    def __init__(self, me, shard):
        core, row = me % 2, me // 2
        self.me = me
        self.core_at = me + 1 - 2 * core
        self.row_at = me + 2 - 4 * row
        self.both_at = self.row_at + 1 - 2 * core
        self.core, self.row, self.both = (
            (at, shard) for at in (self.core_at, self.row_at, self.both_at)
        )
        self.all = (self.core, self.row, self.both)


class TokenSum:
    def __init__(self, around, parts, own_part, row_part, from_core, from_row, send, recv):
        self.around, self.parts, self.own_part, self.row_part = around, parts, own_part, row_part
        self.from_core, self.from_row, self.send, self.recv = from_core, from_row, send, recv

    def loads(self):
        at = self.around
        return (
            (self.parts.at[at.row_at], self.row_part),
            (self.parts.at[at.me], self.own_part),
        )

    def to_core(self, which):
        at = self.around
        return remote(
            self.parts.at[(at.core_at, at.both_at)[which]],
            self.from_core.at[which],
            self.send.at[which],
            self.recv.at[which],
            at.core,
        )

    def to_row(self):
        return remote(
            self.row_part, self.from_row, self.send.at[2], self.recv.at[2], self.around.row
        )

    def start(self):
        self.to_core(1).start()
        self.to_core(0).start()

    def pass_row(self):
        self.to_core(1).wait()
        total = self.row_part[...].astype(F32) + self.from_core[1].astype(F32)
        self.row_part[...] = total.astype(BF16)
        self.to_row().start()

    def total(self):
        self.to_core(0).wait()
        self.to_row().wait()
        return (
            self.own_part[...].astype(F32)
            + self.from_core[0].astype(F32)
            + self.from_row[...].astype(F32)
        )


class SmallSum:
    def __init__(self, n, around, whole, sums, send, recv, ctx_send, ctx_recv):
        self.n, self.around, self.whole, self.sums = n, around, whole, sums
        self.send, self.recv, self.ctx_send, self.ctx_recv = send, recv, ctx_send, ctx_recv
        self.shard = lax.axis_index("fsdp")

    def to_peer(self, offset):
        own = self.whole.at[self.shard]
        peer = (self.around.me, lax.rem(self.shard + offset, self.n))
        return remote(own, own, self.send.at[offset - 1], self.recv.at[offset - 1], peer)

    def to_ctx(self, i):
        own = self.sums.at[self.around.me]
        return remote(own, own, self.ctx_send.at[i], self.ctx_recv.at[i], self.around.all[i])

    def start(self):
        lax.fori_loop(1, self.n, lambda j, carry: (self.to_peer(j).start(), carry)[1], 0)

    def add(self):
        lax.fori_loop(1, self.n, lambda j, carry: (self.to_peer(j).wait(), carry)[1], 0)
        self.sums[self.around.me] = jnp.sum(self.whole[...], axis=0)
        for i in range(3):
            self.to_ctx(i).start()

    def finish(self):
        for i in range(3):
            self.to_ctx(i).wait()


def gate_kernel(
    heads,
    channels,
    length_ref,
    stats,
    pz_ref,
    y_ref,
    dyn_ref,
    w_o,
    gate_gain_ref,
    ynt_ref,
    mixed_ref,
    dz_ref,
    dssd_ref,
    gain_ref,
    stat_all,
    columns,
    v_y,
    v_o,
    load_sem,
    stat_send,
    stat_recv,
):
    block = pl.program_id(0)
    me = lax.axis_index("ctx")
    around = Around(me, lax.axis_index("fsdp"))
    load = pltpu.make_async_copy(w_o, v_o, load_sem.at[0])

    @pl.when(block == 0)
    def _():
        for device in around.all:
            greet(device)
        load.start()
        own = pltpu.make_async_copy(stats, stat_all.at[me], load_sem.at[1])
        own.start()
        own.wait()
        pl.semaphore_wait(pltpu.get_barrier_semaphore(), 3)
        copies = [
            remote(stat_all.at[me], stat_all.at[me], stat_send.at[i], stat_recv.at[i], device)
            for i, device in enumerate(around.all)
        ]
        for copy in copies:
            copy.start()
        for copy in copies:
            copy.wait()
        total = jnp.sum(stat_all[...], axis=0)
        for i in range(total.shape[1] // BLOCK):
            columns[i] = total[:, i * BLOCK : (i + 1) * BLOCK].T
        gain_ref[...] = jnp.zeros_like(gain_ref)
        load.wait()

    valid = column_valid(length_ref, block)
    sums = columns[block]
    scale = lax.rsqrt(sums[:, 0:1] / channels + EPS)
    slant = scale * scale * scale * sums[:, 1:2] / channels
    for first in range(0, heads, 2):
        lanes = slice(first * HEAD, (first + 2) * HEAD)
        gate, gate_slope = silu_and_slope(pz_ref[:, lanes].astype(F32))
        mixed = y_ref[:, lanes]
        d_yn = dyn_ref[:, lanes]
        gain = gate_gain_ref[:, lanes]
        gated = mixed * gate
        scaled = gated * scale
        v_y[:, lanes] = (valid * (scaled * gain)).astype(BF16)
        gain_ref[0:1, lanes] += jnp.sum(d_yn * scaled, axis=0, keepdims=True)
        d_gated = scale * (gain * d_yn) - gated * slant
        dz_ref[:, lanes] = (d_gated * mixed * gate_slope).astype(BF16)
        dssd_ref[:, lanes] = (d_gated * gate).astype(BF16)
    normed_gate = v_y[...]
    ynt_ref[...] = normed_gate.T
    mixed_ref[0] = mm(normed_gate, v_o[...]).astype(BF16)


def gate_norm(channels, length, stats, pz, y, d_yn, w_o, gate_gain):
    tokens, width = pz.shape
    count, model = tokens // BLOCK, w_o.shape[1]
    n_ctx = channels // width
    at_block = lambda size: pl.BlockSpec((BLOCK, size), lambda i: (i, 0))
    any_space = pl.BlockSpec(memory_space=pl.ANY)
    low = lambda *shape: jax.ShapeDtypeStruct(shape, BF16)
    return pl.pallas_call(
        functools.partial(gate_kernel, width // HEAD, channels),
        grid=(count,),
        in_specs=[
            pl.BlockSpec(memory_space=pltpu.SMEM),
            any_space,
            at_block(width),
            at_block(width),
            at_block(width),
            any_space,
            pl.BlockSpec(gate_gain.shape, lambda i: (0, 0)),
        ],
        out_specs=[
            pl.BlockSpec((width, BLOCK), lambda i: (0, i)),
            pl.BlockSpec((1, BLOCK, model), lambda i: (i, 0, 0)),
            at_block(width),
            at_block(width),
            pl.BlockSpec((8, width), lambda i: (0, 0)),
        ],
        out_shape=[
            low(width, tokens),
            low(count, BLOCK, model),
            low(tokens, width),
            low(tokens, width),
            jax.ShapeDtypeStruct((8, width), F32),
        ],
        scratch_shapes=[
            pltpu.VMEM((n_ctx, 8, tokens), F32),
            pltpu.VMEM((count, BLOCK, 8), F32),
            pltpu.VMEM((BLOCK, width), BF16),
            pltpu.VMEM(w_o.shape, BF16),
            pltpu.SemaphoreType.DMA((2,)),
            pltpu.SemaphoreType.DMA((3,)),
            pltpu.SemaphoreType.DMA((3,)),
        ],
        compiler_params=pltpu.CompilerParams(
            collective_id=2, has_side_effects=True, vmem_limit_bytes=56 * 1024 * 1024
        ),
        name="gate_norm",
    )(length, stats, pz, y, d_yn, w_o, gate_gain)


def backward_kernel(
    heads,
    unit,
    n_ctx,
    n,
    px_ref,
    ps_ref,
    x_ref,
    b_ref,
    c_ref,
    slope_x_ref,
    slope_s_ref,
    lam_ref,
    step_ref,
    chain_ref,
    kept_ref,
    dssd_ref,
    gate_t,
    normed_t,
    upstream,
    d_z,
    mixed_parts,
    hidden,
    gain_grads_ref,
    taps_x_ref,
    taps_s_ref,
    skip_ref,
    head_ref,
    dx_ref,
    ds_ref,
    small_ref,
    shard_o,
    shard_z,
    layer_out,
    back,
    mixed_grads,
    for_step,
    for_level,
    left,
    right,
    sums,
    after_x,
    after_s,
    v_left,
    v_right,
    products,
    slots,
    stage,
    done_o,
    done_z,
    mine,
    from_core,
    from_row,
    v_hidden,
    load_sem,
    store_sem,
    ring_send,
    ring_recv,
    part_send,
    part_recv,
):
    turn = pl.program_id(0)
    turns = heads // 2 // POINTS
    block = pl.num_programs(0) - 1 - turn
    width, model = x_ref.shape[1], v_hidden.shape[1]
    own = hidden.shape[0]
    ring = Ring(n)
    around = Around(ring.me, ring.shard)
    piece, size = slots.shape[4], slots.shape[5]
    sum_mixed = TokenSum(
        around, mixed_parts, mine.at[0], mine.at[1], from_core, from_row, part_send, part_recv
    )
    loads = [
        pltpu.make_async_copy(source, target, load_sem.at[i])
        for i, (source, target) in enumerate(
            (
                (gate_t, v_left.at[pl.ds(0, width)]),
                *((upstream.at[c], v_right.at[pl.ds(c * own, own), pl.ds(0, model)]) for c in range(n_ctx)),
                *((normed_t.at[c], v_left.at[pl.ds(width, model), pl.ds(c * own, own)]) for c in range(n_ctx)),
                (d_z, v_right.at[:, pl.ds(model, width)]),
                *sum_mixed.loads(),
                (hidden, v_hidden),
            )
        )
    ]
    ring_loads = 2 + 2 * n_ctx

    def partial_sum(kind, way, sub, index):
        first = (1 - kind) * index * piece + kind * (width + (2 * index + way) * piece)
        at = (1 - kind) * (2 * way + sub) * size + kind * (model + sub * size)
        return mm(
            v_left[pl.ds(pl.multiple_of(first, 16), piece), :],
            v_right[:, pl.ds(pl.multiple_of(at, LANES), size)],
        )

    def all_products():
        tile = max(2 * piece, BLOCK)
        shards = tile // (2 * piece)

        def out_rows(i, carry):
            rows = pl.ds(pl.multiple_of(i * BLOCK, BLOCK), BLOCK)
            left = v_left[rows, :]
            products[rows, 0:width] = mm(left, v_right[:, 0:width]).astype(BF16)
            products[rows, width:model] = mm(left, v_right[:, width:model]).astype(BF16)
            return carry

        def in_rows(i, carry):
            left = v_left[pl.ds(pl.multiple_of(width + i * tile, 16), tile), :]
            both = mm(left, v_right[:, model:]).astype(BF16)
            for j in range(shards):
                place = pl.ds(pl.multiple_of((i * shards + j) * piece, 16), piece)
                for way in (0, 1):
                    products[place, model + way * width : model + (way + 1) * width] = both[
                        (2 * j + way) * piece : (2 * j + way + 1) * piece
                    ]
            return carry

        lax.fori_loop(0, width // BLOCK, out_rows, 0)
        lax.fori_loop(0, model // tile, in_rows, 0)

    def product(kind, way, sub, index):
        at = pl.multiple_of(kind * model + way * width + sub * size, LANES)
        return products[pl.ds(pl.multiple_of(index * piece, 16), piece), pl.ds(at, size)]

    def hop(kind, way, sub, step, source):
        return remote(
            source,
            slots.at[kind, step, way, sub],
            ring_send.at[kind, way, sub],
            ring_recv.at[kind, way, sub, step],
            (ring.me, ring.at(1 - 2 * way)),
        )

    def streams(body):
        def one(e, carry):
            body(e // 4, e // 2 % 2, e % 2)
            return carry

        lax.fori_loop(0, 8, one, 0)

    def start_ring(kind, way, sub):
        place = stage.at[kind, way, sub]
        place[...] = partial_sum(kind, way, sub, ring.at(2 * way - 1)).astype(BF16)
        hop(kind, way, sub, 0, place).start()

    def ring_step(step):
        def body(kind, way, sub):
            index = ring.at((step + 2) * (2 * way - 1))
            hop(kind, way, sub, step, stage.at[kind, way, sub]).wait()
            place = slots.at[kind, step, way, sub]
            total = place[...].astype(F32) + product(kind, way, sub, index).astype(F32)

            @pl.when(step < n - 2)
            def _():
                place[...] = total.astype(BF16)
                hop(kind, way, sub, step + 1, place).start()

            @pl.when(jnp.logical_and(step == n - 2, kind == 0))
            def _():
                at = pl.multiple_of((2 * way + sub) * size, LANES)
                done_o[:, pl.ds(at, size)] = total.astype(BF16)

            @pl.when(jnp.logical_and(step == n - 2, kind == 1))
            def _():
                done_z[way, pl.ds(pl.multiple_of(sub * size, 16), size), :] = total.T.astype(BF16)

        streams(body)

    def serve(point):
        at = turn * POINTS + point
        points = POINTS * n_ctx
        lax.fori_loop(
            at * (n - 1) // points,
            (at + 1) * (n - 1) // points,
            lambda step, carry: (ring_step(step), carry)[1],
            0,
        )

    @pl.when(turn == 0)
    def _():
        for device in around.all:
            greet(device)
        greet(ring.neighbour(0))
        greet(ring.neighbour(1))
        for copy in loads:
            copy.start()
        back[...] = jnp.zeros_like(back)
        small_ref[...] = jnp.zeros_like(small_ref)
        small_ref[taps_x_ref.shape[0] : taps_x_ref.shape[0] + 1, 0:width] = gain_grads_ref[0:1, :]
        after_x[...] = jnp.zeros_like(after_x)
        after_s[...] = jnp.zeros_like(after_s)
        pl.semaphore_wait(pltpu.get_barrier_semaphore(), 5)
        for copy in loads[:ring_loads]:
            copy.wait()
        streams(start_ring)
        sum_mixed.start()
        all_products()
        for copy in loads[ring_loads:]:
            copy.wait()

    @pl.when(turn == 1)
    def _():
        sum_mixed.pass_row()

    taps = taps_x_ref.shape[0] - 1

    rows_b, rows_c = b_ref[...], c_ref[...]
    step = step_ref[...]
    lam = lam_ref[...]
    gram = mm(rows_c, rows_b, ((1,), (1,)))
    gram_t = mm(rows_b, rows_c, ((1,), (1,)))
    level, across, last, weight, fade = levels(lam, step)
    out_decay = jnp.exp(level - level[BLOCK - 1 : BLOCK, :])
    step_across = step.T
    at_row, at_col = iota2((BLOCK, BLOCK), 0), iota2((BLOCK, BLOCK), 1)
    order = (at_row > at_col).astype(F32) - (at_row < at_col).astype(F32)
    low_half = iota2((1, LANES), 1) < HEAD
    lane = iota2((1, LANES), 1)
    by_state = rows_c.T
    kept = kept_ref[0]
    old_back = back[...].astype(BF16)
    entering = mm(rows_c, kept)
    leaving = mm(rows_b, old_back)
    at_last = jnp.sum(kept.astype(F32) * back[...], axis=0, keepdims=True)
    mixed_grads[...] = jnp.zeros_like(mixed_grads)
    left[...] = jnp.zeros_like(left)
    right[...] = jnp.zeros_like(right)
    sums[...] = jnp.zeros_like(sums)
    d_b = jnp.zeros((BLOCK, STATE), F32)
    d_c = jnp.zeros((BLOCK, STATE), F32)

    def conv_back(d_conv, after, current, weight):
        padded = jnp.concatenate([d_conv, after], axis=0)
        d_in = jnp.zeros_like(d_conv)
        grads = []
        for k in range(taps):
            moved = padded[taps - 1 - k : taps - 1 - k + BLOCK]
            d_in += weight[k : k + 1] * moved
            grads.append(jnp.sum(current * moved, axis=0, keepdims=True))
        grads.append(jnp.sum(d_conv, axis=0, keepdims=True))
        return d_in, jnp.concatenate(grads, axis=0)

    for first in range(0, heads, 2):
        lanes = slice(first * HEAD, (first + 2) * HEAD)
        x_low = x_ref[:, lanes]
        x = x_low.astype(F32)
        grad_low = dssd_ref[:, lanes]
        grad = grad_low.astype(F32)
        through = jnp.zeros((BLOCK, LANES), F32)
        for head, keep in ((first, low_half), (first + 1, jnp.logical_not(low_half))):
            decay = spread(level, across, head)
            grad_own = jnp.where(keep, grad, 0.0).astype(BF16)
            pairs = mm(grad_own, x_low, ((1,), (1,)))
            through += mm((gram_t * decay).astype(BF16), grad_own)
            scaled = decay * pairs * step_across[head : head + 1, :]
            mixed_grads[...] += scaled
            ordered = gram * scaled * order
            left[...] = jnp.where(
                lane == head, jnp.sum(ordered, axis=1, keepdims=True), left[...]
            )
            right[head : head + 1, :] = jnp.sum(ordered, axis=0, keepdims=True)
        weight_pair = pair_of(weight, first, low_half)
        step_pair = pair_of(step, first, low_half)
        fade_pair = pair_of(fade, first, low_half)
        out_pair = pair_of(out_decay, first, low_half)
        leave = leaving[:, lanes]
        d_x = step_pair * through + weight_pair * leave + skip_ref[:, lanes] * grad
        for_step[:, lanes] = x * (through + out_pair * leave)
        weighted = weight_pair * x
        faded = fade_pair * grad
        for_level[:, lanes] = weighted * leave - faded * entering[:, lanes]
        sums[0:1, lanes] = jnp.sum(weighted * leave, axis=0, keepdims=True)
        sums[2:3, lanes] = jnp.sum(x * grad, axis=0, keepdims=True)
        faded_low = faded.astype(BF16)
        d_b += mm(weighted.astype(BF16), old_back[:, lanes], ((1,), (1,)))
        d_c += mm(faded_low, kept[:, lanes], ((1,), (1,)))
        back[:, lanes] = back[:, lanes] * pair_of(last, first, low_half) + mm(by_state, faded_low)
        d_conv = d_x * slope_x_ref[:, lanes].astype(F32)
        d_in, grads = conv_back(
            d_conv, after_x[:, lanes], px_ref[:, lanes].astype(F32), taps_x_ref[:, lanes]
        )
        after_x[:, lanes] = d_conv[0:8]
        dx_ref[:, lanes] = d_in.astype(BF16)
        small_ref[0 : taps + 1, lanes] += grads
        if first // 2 % turns == turns - 1 and first // 2 // turns < POINTS - 1:
            serve(first // 2 // turns)

    all_pairs = mixed_grads[...]
    d_b = d_b + mm(all_pairs.T.astype(BF16), rows_c)
    d_c = d_c + mm(all_pairs.astype(BF16), rows_b)
    d_conv = jnp.concatenate([d_b, d_c], axis=1) * slope_s_ref[...].astype(F32)
    d_in, grads = conv_back(
        d_conv, after_s[...], ps_ref[:, : 2 * STATE].astype(F32), taps_s_ref[...]
    )
    after_s[...] = d_conv[0:8]
    ds_ref[:, : 2 * STATE] = d_in.astype(BF16)
    small_ref[0 : taps + 1, width:] += grads

    chooser = (iota2((width, LANES), 0) // HEAD == iota2((width, LANES), 1)).astype(BF16)
    d_step = head_sums(for_step[...], chooser)
    sums[1:2, :] = at_last
    total = head_sums(sums[...], chooser)
    d_level = head_sums(for_level[...], chooser) - left[...] + right[...].T
    final = -total[0:1, :] - last * total[1:2, :]
    d_level = d_level + jnp.where(iota2((BLOCK, 1), 0) == BLOCK - 1, final, 0.0)
    d_lam = mm_exact((at_row <= at_col).astype(F32), d_level)
    d_raw = (d_step + d_lam * head_ref[1:2]) * chain_ref[...]
    head_row = taps + 2
    small_ref[head_row : head_row + 1, 0:LANES] += jnp.sum(d_raw, axis=0, keepdims=True)
    small_ref[head_row : head_row + 1, LANES : 2 * LANES] += jnp.sum(
        d_lam * lam, axis=0, keepdims=True
    )
    small_ref[head_row : head_row + 1, 2 * LANES : 3 * LANES] += total[2:3, :]
    chosen = chosen_heads(lax.axis_index("ctx"), heads, unit, n_ctx, True)
    ds_ref[:, 2 * STATE :] = mm(d_raw.astype(BF16), chosen).astype(BF16)

    serve(POINTS - 1)

    @pl.when(turn == pl.num_programs(0) - 1)
    def _():
        stores = [
            pltpu.make_async_copy(source, target, store_sem.at[i])
            for i, (source, target) in enumerate(
                ((done_o, shard_o), (done_z, shard_z), (v_hidden, layer_out))
            )
        ]
        stores[0].start()
        stores[1].start()
        v_hidden[...] = (v_hidden[...].astype(F32) + sum_mixed.total()).astype(BF16)
        stores[2].start()
        for copy in stores:
            copy.wait()


def scan_backward(
    n, unit, n_ctx, px, ps, kept_parts, d_ssd, gate_t, normed_t, upstream, d_z, mixed_parts, hidden, gain_grads, taps_x, taps_s, skip, head
):
    x, rows_b, rows_c, slope_x, slope_s, lam, step, chain, kept = kept_parts
    tokens, width = px.shape
    heads = width // HEAD
    count = tokens // BLOCK
    own, model = hidden.shape
    shared_width = ps.shape[1]
    piece = width // n
    assert model == 2 * width and heads // 2 % POINTS == 0
    by_block = lambda i: (count - 1 - i, 0)
    at_block = lambda size: pl.BlockSpec((BLOCK, size), by_block)
    whole = lambda a: pl.BlockSpec(a.shape, lambda i: (0, 0))
    any_space = pl.BlockSpec(memory_space=pl.ANY)
    low = lambda *shape: jax.ShapeDtypeStruct(shape, BF16)
    v_low = lambda *shape: pltpu.VMEM(shape, BF16)
    v_full = lambda *shape: pltpu.VMEM(shape, F32)
    part = lambda a, b: pl.BlockSpec((1, a, b), lambda i: (count - 1 - i, 0, 0))
    small_shape = (8, width + 2 * STATE)
    dma = pltpu.SemaphoreType.DMA
    return pl.pallas_call(
        functools.partial(backward_kernel, heads, unit, n_ctx, n),
        grid=(count,),
        in_specs=[
            at_block(width),
            at_block(shared_width),
            at_block(width),
            at_block(STATE),
            at_block(STATE),
            at_block(width),
            at_block(2 * STATE),
            at_block(LANES),
            at_block(LANES),
            at_block(LANES),
            part(STATE, width),
            at_block(width),
        ]
        + [any_space] * 6
        + [whole(a) for a in (gain_grads, taps_x, taps_s, skip, head)],
        out_specs=[
            at_block(width),
            at_block(shared_width),
            pl.BlockSpec(small_shape, lambda i: (0, 0)),
            any_space,
            any_space,
            any_space,
        ],
        out_shape=[
            low(tokens, width),
            low(tokens, shared_width),
            jax.ShapeDtypeStruct(small_shape, F32),
            low(piece, model),
            low(2, width, piece),
            low(own, model),
        ],
        scratch_shapes=[
            v_full(STATE, width),
            v_full(BLOCK, BLOCK),
            v_full(BLOCK, width),
            v_full(BLOCK, width),
            v_full(BLOCK, LANES),
            v_full(LANES, BLOCK),
            v_full(8, width),
            v_full(8, width),
            v_full(8, 2 * STATE),
            v_low(width + model, tokens),
            v_low(tokens, model + width),
            v_low(width, 2 * model),
            v_low(2, n - 1, 2, 2, piece, width // 2),
            v_low(2, 2, 2, piece, width // 2),
            v_low(piece, model),
            v_low(2, width, piece),
            v_low(2, own, model),
            v_low(2, own, model),
            v_low(own, model),
            v_low(own, model),
            dma((5 + 2 * n_ctx,)),
            dma((3,)),
            dma((2, 2, 2)),
            dma((2, 2, 2, n - 1)),
            dma((3,)),
            dma((3,)),
        ],
        compiler_params=pltpu.CompilerParams(
            collective_id=3, has_side_effects=True, vmem_limit_bytes=59 * 1024 * 1024
        ),
        name="scan_backward",
    )(
        px, ps, x, rows_b, rows_c, slope_x, slope_s, lam, step, chain, kept, d_ssd, gate_t, normed_t, upstream, d_z, mixed_parts, hidden, gain_grads, taps_x, taps_s, skip, head
    )


def gather_kernel(
    n,
    n_ctx,
    unit,
    direct,
    hidden,
    cotangent,
    in_weight_t,
    small,
    out_weight,
    cotangent_all,
    w_x,
    w_s,
    w_z,
    w_o,
    small_out,
    proj_x,
    proj_s,
    proj_z,
    normed_t,
    v_hidden,
    v_normed,
    v_x,
    v_s,
    v_z,
    v_small,
    raw_x,
    raw_s,
    raw_z,
    out_x,
    out_s,
    out_z,
    out_t,
    v_gain,
    load_sem,
    column_sem,
    local_sem,
    store_sem,
    ring_send,
    ring_recv,
    ctx_send,
    ctx_recv,
    piece_send,
    piece_recv,
):
    ring = Ring(n)
    me, shard = ring.me, ring.shard
    width, model = v_x.shape[1], v_x.shape[0]
    inner = width * n_ctx
    r = model // n
    shared = in_weight_t.shape[0] - 2 * inner
    row = me // 2
    other_core = (me + 1 - 2 * (me % 2), shard)
    other_row = (me + 2 - 4 * row, shard)
    piece = w_o.shape[1]
    piece_peer = (shard % n_ctx, shard // n_ctx * n_ctx + me)
    moves = shard % n_ctx != me

    barrier = pltpu.get_barrier_semaphore()
    for device in (other_core, other_row, ring.neighbour(0), ring.neighbour(1)):
        pl.semaphore_signal(barrier, inc=1, device_id=device, device_id_type=MESH)

    part = unit * HEAD

    def load_columns(base, target, sems):
        return [
            pltpu.make_async_copy(
                in_weight_t.at[pl.ds(pl.multiple_of(base + (a * n_ctx + me) * part, 16), part)],
                target.at[pl.ds(a * part, part)],
                sems.at[a],
            )
            for a in range(width // part)
        ]

    loads = [
        load_columns(inner, raw_x, column_sem.at[0]),
        [
            pltpu.make_async_copy(
                in_weight_t.at[pl.ds(2 * inner, shared)], raw_s.at[pl.ds(0, shared)], load_sem.at[0]
            )
        ],
        [pltpu.make_async_copy(small, v_small.at[shard], load_sem.at[1])],
        [pltpu.make_async_copy(hidden, v_hidden.at[me], load_sem.at[2])],
        load_columns(0, raw_z, column_sem.at[1]),
    ]
    for copies in loads:
        for copy in copies:
            copy.start()

    def loaded(i):
        for copy in loads[i]:
            copy.wait()

    if direct:
        pl.semaphore_wait(barrier, 4)
    else:

        @pl.when(moves)
        def _():
            pl.semaphore_signal(barrier, inc=1, device_id=piece_peer, device_id_type=MESH)
            pl.semaphore_wait(barrier, 5)

        @pl.when(jnp.logical_not(moves))
        def _():
            pl.semaphore_wait(barrier, 4)

    half, quarter = width // 2, w_o.shape[2] // 4
    rows = r // 2
    both_rows = lambda index, way: pl.ds(pl.multiple_of((2 * index + way) * rows, 16), rows)
    x_part = lambda a, sub: lambda index, way: a.at[both_rows(index, way), pl.ds(sub * half, half)]
    s_part = lambda index, way: v_s.at[both_rows(index, way)]
    small_part = lambda index, way: v_small.at[index, pl.ds(way * SMALL_ROWS // 2, SMALL_ROWS // 2)]
    o_part = lambda sub: lambda index, way: w_o.at[
        index, :, pl.ds((2 * way + sub) * quarter, quarter)
    ]
    phases = (
        ((0, small_part), (1, s_part), (2, x_part(v_x, 0)), (3, x_part(v_x, 1))),
        ((4, x_part(v_z, 0)), (5, x_part(v_z, 1))),
        ((6, o_part(0)), (7, o_part(1))),
    )

    def hop(stream, way, step):
        number, part = stream
        place = part(ring.at(-step if way == 0 else step), way)
        return remote(
            place, place, ring_send.at[number, way], ring_recv.at[number, way, step],
            ring.neighbour(way),
        )

    def arrives(stream, way, step):
        number, part = stream
        landed = part(ring.at(-step - 1 if way == 0 else step + 1), way)
        return remote(
            landed, landed, ring_send.at[number, way], ring_recv.at[number, way, step],
            ring.neighbour(way),
        )

    def start_stream(stream):
        for way in (0, 1):
            hop(stream, way, 0).start()

    def to_row(i, a, whole):
        return remote(a, whole.at[me], ctx_send.at[i, 0], ctx_recv.at[i, 0], other_row)

    def to_core(i, a, whole):
        return remote(a, whole.at[me], ctx_send.at[i, 1], ctx_recv.at[i, 1], other_core)

    def pass_on(i, whole):
        beyond = whole.at[other_row[0]]
        return remote(beyond, beyond, ctx_send.at[i, 2], ctx_recv.at[i, 2], other_core)

    to_row(0, hidden, v_hidden).start()
    to_core(0, hidden, v_hidden).start()
    own_rows = pl.ds(pl.multiple_of(shard * r, 16), r)
    loaded(2)
    start_stream(phases[0][0])
    loaded(0)
    v_x[own_rows, :] = raw_x[...].T
    start_stream(phases[0][2])
    start_stream(phases[0][3])
    loaded(1)
    raw_s[shared:, :] = jnp.zeros((raw_s.shape[0] - shared, r), BF16)
    v_s[own_rows, :] = raw_s[...].T
    start_stream(phases[0][1])
    own_piece = out_weight.at[pl.ds(pl.multiple_of(me * piece, 16), piece)]
    keep_piece = pltpu.make_async_copy(own_piece, w_o.at[shard], piece_send)

    def move_piece(wait):
        if direct:
            keep_piece.wait() if wait else keep_piece.start()
            return
        send_piece = remote(own_piece, w_o.at[piece_peer[1]], piece_send, piece_recv, piece_peer)

        @pl.when(moves)
        def _():
            send_piece.wait() if wait else send_piece.start()

        @pl.when(jnp.logical_not(moves))
        def _():
            keep_piece.wait() if wait else keep_piece.start()

    keep_cotangent = pltpu.make_async_copy(cotangent, cotangent_all.at[me], local_sem)
    keep_cotangent.start()
    loaded(3)
    loaded(4)
    v_z[own_rows, :] = raw_z[...].T

    def run_phase(number, work, after):
        def body(step, carry):
            for stream in phases[number]:
                for way in (0, 1):
                    arrives(stream, way, step).wait_recv()
                    hop(stream, way, step).wait_send()
                    hop(stream, way, step + 1).start()
            if work is not None:

                @pl.when(step < n_ctx)
                def _():
                    work(step)

            return carry

        lax.fori_loop(0, n - 2, body, 0)
        after()
        for stream in phases[number]:
            for way in (0, 1):
                arrives(stream, way, n - 2).wait_recv()
                hop(stream, way, n - 2).wait_send()

    tokens = v_hidden.shape[1]

    def project_first(chunk):
        at = pl.ds(pl.multiple_of(chunk * tokens, tokens), tokens)
        resid = v_hidden[chunk].astype(F32)
        scale = lax.rsqrt(jnp.mean(resid * resid, axis=1, keepdims=True) + EPS)
        normed = (resid * scale * v_gain[...]).astype(BF16)
        v_normed[at, :] = normed
        out_x[at, :] = mm(normed, v_x[...]).astype(BF16)
        out_s[at, :] = mm(normed, v_s[...]).astype(BF16)

    def project_gate(chunk):
        at = pl.ds(pl.multiple_of(chunk * tokens, tokens), tokens)
        normed = v_normed[at, :]
        out_z[at, :] = mm(normed, v_z[...]).astype(BF16)
        out_t[chunk] = normed.T

    stores = [
        pltpu.make_async_copy(source, target, store_sem.at[i])
        for i, (source, target) in enumerate(
            (
                (v_x, w_x),
                (v_s, w_s),
                (v_small, small_out),
                (out_x, proj_x),
                (out_s, proj_s),
                (v_z, w_z),
                (out_z, proj_z),
                (out_t, normed_t),
            )
        )
    ]

    def after_first():
        for stream in phases[1]:
            start_stream(stream)
        to_row(0, hidden, v_hidden).wait_recv()
        pass_on(0, v_hidden).start()
        move_piece(False)
        to_row(1, cotangent, cotangent_all).start()
        to_core(1, cotangent, cotangent_all).start()
        to_row(0, hidden, v_hidden).wait_send()
        to_core(0, hidden, v_hidden).wait()
        pass_on(0, v_hidden).wait()

    def after_second():
        move_piece(True)
        for stream in phases[2]:
            start_stream(stream)
        to_row(1, cotangent, cotangent_all).wait_recv()
        pass_on(1, cotangent_all).start()

    def after_third():
        to_row(1, cotangent, cotangent_all).wait_send()
        to_core(1, cotangent, cotangent_all).wait()
        pass_on(1, cotangent_all).wait()
        keep_cotangent.wait()

    run_phase(0, None, after_first)
    for f in range(n):
        v_gain[:, f * r : (f + 1) * r] = v_small[f, 0:1, 0:r].astype(F32)
    for copy in stores[0:3]:
        copy.start()
    run_phase(1, project_first, after_second)
    for copy in stores[3:6]:
        copy.start()
    run_phase(2, project_gate, after_third)
    for copy in stores[6:]:
        copy.start()
    for copy in stores:
        copy.wait()


def gather_all(n, n_ctx, unit, direct, hidden, cotangent, in_weight_t, small, out_weight, shared_width):
    own, model = hidden.shape
    tokens = own * n_ctx
    width = out_weight.shape[0] * n // n_ctx
    rows = in_weight_t.shape[1]
    any_space = pl.BlockSpec(memory_space=pl.ANY)
    low = lambda *shape: jax.ShapeDtypeStruct(shape, BF16)
    v_low = lambda *shape: pltpu.VMEM(shape, BF16)
    dma = pltpu.SemaphoreType.DMA
    return pl.pallas_call(
        functools.partial(gather_kernel, n, n_ctx, unit, direct),
        in_specs=[any_space] * 5,
        out_specs=[any_space] * 10,
        out_shape=[
            low(n_ctx, own, model),
            low(model, width),
            low(model, shared_width),
            low(model, width),
            low(n, width // n, model),
            low(n, small.shape[0], small.shape[1]),
            low(tokens, width),
            low(tokens, shared_width),
            low(tokens, width),
            low(n_ctx, model, own),
        ],
        scratch_shapes=[
            v_low(n_ctx, own, model),
            v_low(tokens, model),
            v_low(model, width),
            v_low(model, shared_width),
            v_low(model, width),
            v_low(n, small.shape[0], small.shape[1]),
            v_low(width, rows),
            v_low(shared_width, rows),
            v_low(width, rows),
            v_low(tokens, width),
            v_low(tokens, shared_width),
            v_low(tokens, width),
            v_low(n_ctx, model, own),
            pltpu.VMEM((1, model), F32),
            dma((3,)),
            dma((2, width // (unit * HEAD))),
            dma,
            dma((8,)),
            dma((8, 2)),
            dma((8, 2, n - 1)),
            dma((2, 3)),
            dma((2, 3)),
            dma,
            dma,
        ],
        compiler_params=pltpu.CompilerParams(
            collective_id=0, has_side_effects=True, vmem_limit_bytes=56 * 1024 * 1024
        ),
        name="gather_all",
    )(hidden, cotangent, in_weight_t, small, out_weight)


def reduce_kernel(
    n,
    n_ctx,
    direct,
    normed_t,
    d_z,
    d_x,
    d_s,
    w_z,
    w_x,
    w_s,
    shard_o,
    shard_z,
    small,
    hidden,
    cotangent,
    gain,
    g_z,
    g_x,
    g_s,
    g_o,
    hidden_grad,
    small_out,
    norm_out,
    v_normed_t,
    v_d_z,
    v_d_x,
    v_d_s,
    v_z,
    v_x,
    v_s,
    parts,
    partials,
    slots,
    stage,
    done,
    moved,
    from_core,
    from_row,
    v_hidden,
    v_cotangent,
    v_gain,
    small_all,
    small_ctx,
    norm_all,
    norm_ctx,
    load_sem,
    store_sem,
    ring_send,
    ring_recv,
    ctx_send,
    ctx_recv,
    own_sem,
    piece_send,
    piece_recv,
    part_send,
    part_recv,
    small_send,
    small_recv,
    small_ctx_send,
    small_ctx_recv,
):
    ring = Ring(n)
    me, shard = ring.me, ring.shard
    around = Around(me, shard)
    core, row = me % 2, me // 2
    piece_peer = (shard % n_ctx, shard // n_ctx * n_ctx + me)
    moves = shard % n_ctx != me
    barrier = pltpu.get_barrier_semaphore()
    for device in around.all:
        greet(device)
    lax.fori_loop(1, n, lambda j, carry: (greet((me, lax.rem(shard + j, n))), carry)[1], 0)
    own = hidden.shape[0]
    sum_normed = TokenSum(
        around, parts, parts.at[me], parts.at[around.row_at], from_core, from_row, part_send, part_recv
    )
    sum_small, sum_norm = (
        SmallSum(
            n, around, whole, sums, small_send.at[i], small_recv.at[i], small_ctx_send.at[i], small_ctx_recv.at[i]
        )
        for i, (whole, sums) in enumerate(((small_all, small_ctx), (norm_all, norm_ctx)))
    )
    loads = [
        pltpu.make_async_copy(source, target, load_sem.at[i])
        for i, (source, target) in enumerate(
            (
                *((normed_t.at[c], v_normed_t.at[:, pl.ds(c * own, own)]) for c in range(n_ctx)),
                (d_s, v_d_s),
                (d_x, v_d_x),
                (small, small_all.at[shard]),
                (d_z, v_d_z),
                (w_z, v_z),
                (w_x, v_x),
                (w_s, v_s),
                (hidden, v_hidden),
                (cotangent, v_cotangent),
                (gain, v_gain),
            )
        )
    ]
    ring_loads = n_ctx + 2
    for copy in loads:
        copy.start()
    if direct:
        pl.semaphore_wait(barrier, n + 2)
    else:

        @pl.when(moves)
        def _():
            greet(piece_peer)
            pl.semaphore_wait(barrier, n + 3)

        @pl.when(jnp.logical_not(moves))
        def _():
            pl.semaphore_wait(barrier, n + 2)

    rows = v_normed_t.shape[0] // (2 * n)
    half, last = v_d_x.shape[1] // 2, v_d_s.shape[1]
    streams = (
        (0, v_d_s, 0, last, 2 * half),
        (1, v_d_x, 0, half, 0),
        (2, v_d_x, half, half, half),
    )

    def compute_partials(step):
        for way in (0, 1):
            index = ring.at(-step - 2 if way == 0 else step + 2)
            left = v_normed_t[pl.ds(pl.multiple_of((2 * index + way) * rows, 16), rows), :]
            partials[way, :, 2 * half :] = mm(left, v_d_s[...])
            partials[way, :, 0 : 2 * half] = mm(left, v_d_x[...])

    def slot(stream, way, step):
        return slots.at[step, way, :, pl.ds(stream[4], stream[3])]

    def hop(stream, way, step, source):
        return remote(
            source,
            slot(stream, way, step),
            ring_send.at[stream[0], way],
            ring_recv.at[stream[0], way, step],
            ring.neighbour(way),
        )

    def first_part(stream, way):
        return stage.at[way, :, pl.ds(stream[4], stream[3])]

    def arrived(stream, way, step):
        hop(stream, way, step, first_part(stream, way)).wait()
        partial = partials[way, :, stream[4] : stream[4] + stream[3]]
        return slot(stream, way, step)[...].astype(F32) + partial

    done_of = lambda stream: done.at[pl.ds(stream[4], stream[3])]
    of_x = lambda c, first: g_x.at[c, pl.ds(first, half)]
    shares = (
        (shard_o if direct else moved, lambda c: g_o.at[c]),
        (shard_z, lambda c: g_z.at[c]),
        (done_of(streams[1]), lambda c: of_x(c, 0)),
        (done_of(streams[2]), lambda c: of_x(c, half)),
        (done_of(streams[0]), lambda c: g_s.at[c]),
    )

    def share(i, kind):
        source, whole = shares[i]
        at = me
        if kind == 2:
            source, at = whole(around.row_at), around.row_at
        device = around.row if kind == 0 else around.core
        return remote(source, whole(at), ctx_send.at[i, kind], ctx_recv.at[i, kind], device)

    def keep(i):
        return pltpu.make_async_copy(shares[i][0], shares[i][1](me), own_sem.at[i])

    def start_share(i):
        share(i, 0).start()
        share(i, 1).start()
        keep(i).start()

    def pass_share(i):
        share(i, 0).wait_recv()
        share(i, 2).start()

    def close_share(i):
        share(i, 0).wait_send()
        share(i, 1).wait()
        share(i, 2).wait()
        keep(i).wait()

    def move_piece(wait):
        if direct:
            return
        keep_piece = pltpu.make_async_copy(shard_o, moved, piece_send)
        send_piece = remote(shard_o, moved, piece_send, piece_recv, piece_peer)

        @pl.when(moves)
        def _():
            send_piece.wait() if wait else send_piece.start()

        @pl.when(jnp.logical_not(moves))
        def _():
            keep_piece.wait() if wait else keep_piece.start()

    def normed_part(i, carry):
        to_row = row + (1 - i % 2) * (1 - 2 * row)
        to_core = core + (1 - i // 2) * (1 - 2 * core)
        at = 2 * to_row + to_core
        tokens = pl.ds(pl.multiple_of(at * own, own), own)
        parts[at] = (
            mm(v_d_z[tokens, :], v_z[...], ((1,), (1,)))
            + mm(v_d_x[tokens, :], v_x[...], ((1,), (1,)))
            + mm(v_d_s[tokens, :], v_s[...], ((1,), (1,)))
        ).astype(BF16)
        return carry

    store_grad = pltpu.make_async_copy(v_cotangent, hidden_grad, store_sem.at[0])
    store_small = pltpu.make_async_copy(small_ctx, small_out, store_sem.at[1])
    store_norm = pltpu.make_async_copy(norm_ctx, norm_out, store_sem.at[2])

    def finish_tokens():
        resid = v_hidden[...].astype(F32)
        scale = lax.rsqrt(jnp.mean(resid * resid, axis=1, keepdims=True) + EPS)
        d_normed = sum_normed.total()
        f = v_gain[...] * d_normed
        slope = scale**3 * jnp.mean(resid * f, axis=1, keepdims=True)
        grad = v_cotangent[...].astype(F32) + scale * f - resid * slope
        v_cotangent[...] = grad.astype(BF16)
        store_grad.start()
        by_model = jnp.sum(d_normed * resid * scale, axis=0, keepdims=True)
        size = norm_all.shape[2]
        for j in range(norm_all.shape[1]):
            norm_all[shard, j : j + 1, :] = by_model[:, j * size : (j + 1) * size]
        sum_norm.start()

    move_piece(False)
    for copy in loads[:ring_loads]:
        copy.wait()
    compute_partials(-1)
    for way in (0, 1):
        stage[way] = partials[way].astype(BF16)
        for stream in streams:
            hop(stream, way, 0, first_part(stream, way)).start()
    compute_partials(0)
    for copy in loads[ring_loads:]:
        copy.wait()
    sum_small.start()
    move_piece(True)
    start_share(0)
    start_share(1)

    def body(step, carry):
        for stream in streams:
            for way in (0, 1):
                total = arrived(stream, way, step)
                place = slot(stream, way, step)
                place[...] = total.astype(BF16)
                hop(stream, way, step + 1, place).start()
        compute_partials(step + 1)

        @pl.when(step < 2)
        def _():
            lax.fori_loop(2 * step, 2 * step + 2, normed_part, 0)

        @pl.when(step == 0)
        def _():
            sum_normed.start()

        @pl.when(step == 1)
        def _():
            sum_normed.pass_row()

        @pl.when(step == n - 3)
        def _():
            finish_tokens()

        return carry

    lax.fori_loop(0, n - 2, body, 0)
    sum_small.add()
    pass_share(0)
    pass_share(1)
    for number, shared in ((0, 4), (1, 2), (2, 3)):
        place = done_of(streams[number])
        for way in (0, 1):
            total = arrived(streams[number], way, n - 2)
            place[:, way * rows : (way + 1) * rows] = total.T.astype(BF16)
        start_share(shared)
    sum_norm.add()
    sum_small.finish()
    store_small.start()
    for i in (4, 2, 3):
        pass_share(i)
    sum_norm.finish()
    store_norm.start()
    for i in range(5):
        close_share(i)
    store_grad.wait()
    store_small.wait()
    store_norm.wait()


def reduce_all(
    n, n_ctx, direct, normed_t, d_z, d_x, d_s, w_z, w_x, w_s, shard_o, shard_z, small, hidden, cotangent, gain
):
    model, tokens = normed_t.shape[1], d_x.shape[0]
    width, shared_width = d_x.shape[1], d_s.shape[1]
    rows, piece, own = model // n, width // n, hidden.shape[0]
    columns = width + shared_width
    any_space = pl.BlockSpec(memory_space=pl.ANY)
    dma = pltpu.SemaphoreType.DMA
    low = lambda *shape: jax.ShapeDtypeStruct(shape, BF16)
    v_low = lambda *shape: pltpu.VMEM(shape, BF16)
    v_full = lambda *shape: pltpu.VMEM(shape, F32)
    norm_shape = (8, model // 8)
    return pl.pallas_call(
        functools.partial(reduce_kernel, n, n_ctx, direct),
        in_specs=[any_space] * 13,
        out_specs=[any_space] * 7,
        out_shape=[
            low(n_ctx, 2, width, rows // 2),
            low(n_ctx, width, rows),
            low(n_ctx, shared_width, rows),
            low(n_ctx, piece, model),
            low(own, model),
            jax.ShapeDtypeStruct((n_ctx,) + small.shape, F32),
            jax.ShapeDtypeStruct((n_ctx,) + norm_shape, F32),
        ],
        scratch_shapes=[
            v_low(model, tokens),
            v_low(tokens, width),
            v_low(tokens, width),
            v_low(tokens, shared_width),
            v_low(*w_z.shape),
            v_low(*w_x.shape),
            v_low(*w_s.shape),
            v_low(n_ctx, own, model),
            v_full(2, rows // 2, columns),
            v_low(n - 1, 2, rows // 2, columns),
            v_low(2, rows // 2, columns),
            v_low(columns, rows),
            v_low(piece, model),
            v_low(2, own, model),
            v_low(own, model),
            v_low(own, model),
            v_low(own, model),
            v_full(1, model),
            v_full(n, *small.shape),
            v_full(n_ctx, *small.shape),
            v_full(n, *norm_shape),
            v_full(n_ctx, *norm_shape),
            dma((10 + n_ctx,)),
            dma((3,)),
            dma((3, 2)),
            dma((3, 2, n - 1)),
            dma((5, 3)),
            dma((5, 3)),
            dma((5,)),
            dma,
            dma,
            dma((3,)),
            dma((3,)),
            dma((2, n - 1)),
            dma((2, n - 1)),
            dma((2, 3)),
            dma((2, 3)),
        ],
        compiler_params=pltpu.CompilerParams(
            collective_id=1, has_side_effects=True, vmem_limit_bytes=58 * 1024 * 1024
        ),
        name="reduce_all",
    )(
        normed_t, d_z, d_x, d_s, w_z, w_x, w_s, shard_o, shard_z, small, hidden, cotangent, gain
    )


def assemble_kernel(part, z_ref, x_ref, s_ref, out_ref):
    place = pl.program_id(0)
    n_ctx, size, half = x_ref.shape[0], x_ref.shape[1], z_ref.shape[3]

    def interleave(write):
        for a in range(size // part):
            for c in range(n_ctx):
                write(
                    slice((a * n_ctx + c) * part, (a * n_ctx + c + 1) * part),
                    c,
                    slice(a * part, (a + 1) * part),
                )

    def write_z(target, c, source):
        for way in (0, 1):
            out_ref[target, way * half : (way + 1) * half] = z_ref[c, way, source, :].astype(F32)

    def write_x(target, c, source):
        out_ref[target, :] = x_ref[c, source, :].astype(F32)

    @pl.when(place < n_ctx)
    def _():
        interleave(write_z)

    @pl.when(jnp.logical_and(place >= n_ctx, place < 2 * n_ctx))
    def _():
        interleave(write_x)

    @pl.when(place == 2 * n_ctx)
    def _():
        total = s_ref[0].astype(F32)
        for c in range(1, n_ctx):
            total += s_ref[c].astype(F32)
        out_ref[0 : total.shape[0], :] = total


def assemble(part, g_z, g_x, g_s, columns):
    n_ctx, width, rows = g_x.shape
    block = (n_ctx, width // n_ctx, rows)
    return pl.pallas_call(
        functools.partial(assemble_kernel, part),
        grid=(2 * n_ctx + 1,),
        in_specs=[
            pl.BlockSpec(
                (n_ctx, 2, width // n_ctx, rows // 2),
                lambda i: (0, 0, jnp.minimum(i, n_ctx - 1), 0),
            ),
            pl.BlockSpec(block, lambda i: (0, jnp.clip(i - n_ctx, 0, n_ctx - 1), 0)),
            pl.BlockSpec(g_s.shape, lambda i: (0, 0, 0)),
        ],
        out_specs=pl.BlockSpec((width, rows), lambda i: (i, 0)),
        out_shape=jax.ShapeDtypeStruct((columns, rows), F32),
        compiler_params=pltpu.CompilerParams(vmem_limit_bytes=58 * 1024 * 1024),
        name="assemble",
    )(g_z, g_x, g_s)


def on_device(
    hidden,
    cotangent,
    seq_lens,
    norm_gain,
    in_weight,
    conv_weight,
    conv_bias,
    dt_bias,
    a_log,
    d_skip,
    gate_gain,
    out_weight,
):
    n_ctx, n_fsdp = lax.axis_size("ctx"), lax.axis_size("fsdp")
    me, shard = lax.axis_index("ctx"), lax.axis_index("fsdp")
    taps = conv_weight.shape[0]
    heads_all = dt_bias.shape[0] * n_fsdp
    inner = out_weight.shape[0] * n_fsdp
    heads, width = heads_all // n_ctx, inner // n_ctx
    model = hidden.shape[2]
    both = 2 * STATE
    held = dt_bias.shape[0]
    direct = held % n_ctx == 0
    unit = held // n_ctx if direct else 1
    part = unit * HEAD
    shared_width = -(-(both + heads_all) // LANES) * LANES

    per_head = jnp.concatenate([dt_bias, a_log, d_skip])
    lines = [norm_gain[None], conv_weight, conv_bias[None], gate_gain[None], per_head[None]]
    longest = -(-max(a.shape[1] for a in lines) // LANES) * LANES
    small = jnp.concatenate([jnp.pad(a, ((0, 0), (0, longest - a.shape[1]))) for a in lines])
    small = jnp.pad(small, ((0, SMALL_ROWS - small.shape[0]), (0, 0)))
    upstream, w_x, w_s, w_z, w_o, small_all, proj_x, proj_s, proj_z, normed_t = gather_all(
        n_fsdp, n_ctx, unit, direct, hidden[0], cotangent[0], in_weight.T, small, out_weight, shared_width
    )
    w_o = w_o.reshape(-1, model)

    def line(first, count, size):
        rows = small_all[:, first : first + count, :size]
        return jnp.moveaxis(rows, 0, 1).reshape(count, -1).astype(F32)

    def own(lines, size):
        by_part = lines.reshape(lines.shape[0], -1, n_ctx, size)
        return lax.dynamic_index_in_dim(by_part, me, 2, False).reshape(lines.shape[0], -1)

    gain_norm = line(0, 1, norm_gain.shape[0])
    conv_lines = line(1, taps + 1, conv_bias.shape[0])
    taps_x, taps_s = own(conv_lines[:, :inner], part), conv_lines[:, inner:]
    gain_gate = own(line(taps + 2, 1, gate_gain.shape[0]), part)
    each = small_all[:, taps + 3, : per_head.shape[0]].reshape(n_fsdp, 3, -1)
    each = own(jnp.moveaxis(each, 0, 1).reshape(3, -1).astype(F32), unit)
    head = jnp.pad(jnp.stack([each[0], jnp.exp(each[1])]), ((0, 0), (0, LANES - heads)))
    skip = jnp.repeat(each[2], HEAD)[None]

    *kept_parts, y, d_yn, stats = scan_forward(
        unit, n_ctx, seq_lens, proj_x, proj_s, proj_z, upstream, w_o, taps_x, taps_s, gain_gate, skip, head
    )
    gate_t, mixed_parts, d_z, d_ssd, gain_grads = gate_norm(
        inner, seq_lens, stats, proj_z, y, d_yn, w_o, gain_gate
    )
    d_x, d_s, small_grads, shard_o, shard_z, layer_out = scan_backward(
        n_fsdp, unit, n_ctx, proj_x, proj_s, kept_parts, d_ssd, gate_t, normed_t, upstream, d_z, mixed_parts, hidden[0], gain_grads, taps_x, taps_s, skip, head
    )
    g_z, g_x, g_s, g_o, hidden_grad, sums, norm_sums = reduce_all(
        n_fsdp, n_ctx, direct, normed_t, d_z, d_x, d_s, w_z, w_x, w_s, shard_o, shard_z, small_grads, hidden[0], cotangent[0], gain_norm
    )
    grad_in_weight = assemble(part, g_z, g_x, g_s, 2 * inner + both + heads_all).T
    grad_out_weight = g_o.reshape(-1, model).astype(F32)

    def shard_of(lines):
        size = lines.shape[1] // n_fsdp
        return lax.dynamic_slice_in_dim(lines, shard * size, size, axis=1)

    def in_order(sums_of, size):
        lines = sums_of.shape[1]
        by_part = sums_of.reshape(n_ctx, lines, -1, size)
        return jnp.transpose(by_part, (1, 2, 0, 3)).reshape(lines, -1)

    conv_sums = shard_of(
        jnp.concatenate(
            [
                in_order(sums[:, : taps + 1, :width], part),
                jnp.sum(sums[:, : taps + 1, width:], axis=0),
            ],
            axis=1,
        )
    )
    gate_sums = shard_of(in_order(sums[:, taps + 1 : taps + 2, :width], part))
    head_sums_all = sums[:, taps + 2, : 3 * LANES].reshape(n_ctx, 3, LANES)[:, :, :heads]
    head_grads = shard_of(in_order(head_sums_all, unit))
    norm_sums = jnp.sum(norm_sums, axis=0).reshape(1, -1)
    return (
        layer_out[None],
        hidden_grad[None],
        shard_of(norm_sums)[0],
        grad_in_weight,
        conv_sums[:taps],
        conv_sums[taps],
        head_grads[0],
        head_grads[1],
        head_grads[2],
        gate_sums[0],
        grad_out_weight,
    )


def solution(mesh):
    tokens, rows, flat = P("fsdp", "ctx", None), P("fsdp", None), P("fsdp")
    taps = P(None, "fsdp")
    return jax.shard_map(
        on_device,
        mesh=mesh,
        in_specs=(tokens, tokens, flat, flat, rows, taps, flat, flat, flat, flat, flat, rows),
        out_specs=(tokens, tokens, flat, rows, taps, flat, flat, flat, flat, flat, rows),
        check_vma=False,
    )
```

profile of v0, /device:TPU:17, one launch (start us, length us, event | category | flops | bytes accessed | tf_op | source)
XLA Modules:
  0.0 412.9 jit_solution(17443328169316386640)
XLA Ops:
  1.3 0.8 maximum_bitcast_fusion
  2.1 0.7 broadcast_in_dim.21
  2.7 0.7 broadcast_in_dim.23
  3.4 0.7 broadcast_in_dim.22
  4.1 0.7 pad.29
  4.9 0.6 pad.33.small
  5.5 142.6 %gather_all.1 = (bf16[4,256,2048]{2,1,0:T(8,128)(2,1)}, bf16[2048,1024]{1,0:T(8,128)(2,1)}, bf16[2048,384]{1,0:T(8,128)(2,1)}, bf16[2048,1024]{1,0:T(8,128)(2,1)...) custom-call(bf16[256,2048]{1,0:T(8,128)(2,1)} %bitcast.63, ...), custom_call_target="tpu_custom_call" | custom-call | tf_op jit(solution)/shard_map/gather_all/pallas_call | solution.py:1231
  148.1 0.7 convert_reduce_fusion
  148.9 0.8 slice.71
  149.7 0.6 convert.8.gain
  150.3 0.1 copy.40
  150.4 0.1 copy.42
  150.5 0.1 slice.69
  150.6 0.1 copy.41
  150.7 0.1 squeeze.39
  150.8 0.1 copy.43
  150.8 0.1 exp.14
  150.9 0.6 select_maximum_fusion.head_ref
  151.6 0.7 broadcast_in_dim_reshape.3.skip_ref
  152.2 0.9 slice_convert_fusion
  153.1 0.9 convert_bitcast_fusion
  154.0 0.6 dynamic-slice_bitcast_fusion.gate_gain_ref
  154.6 0.1 reshape.129
  154.8 0.6 slice.83.taps_s_ref
  155.5 0.6 copy.57
  156.1 30.0 %scan_forward.1 = (bf16[1024,1024]{1,0:T(8,128)(2,1)}, bf16[1024,128]{1,0:T(8,128)(2,1)}, bf16[1024,128]{1,0:T(8,128)(2,1)}, bf16[1024,1024]{1,0:T(8,128)(2,1)},...) custom-call(s32[1]{0:T(128)S(6)} %copy.61.length_ref, ...), custom_call_target="tpu_custom_call" | custom-call | flops 5905580032 | bytes 25165824 | tf_op jit(solution)/shard_map/scan_forward/pallas_call | solution.py:193
  186.2 20.7 %gate_norm.1 = (bf16[1024,1024]{1,0:T(8,128)(2,1)}, bf16[4,256,2048]{2,1,0:T(8,128)(2,1)}, bf16[1024,1024]{1,0:T(8,128)(2,1)}, bf16[1024,1024]{1,0:T(8,128)(2,1)}, f32[8,1024]{1,0:T(8,128)}) custom-call(s32[1]{0:T(128)S(6)} %copy.61.length_ref, f32[8,1024]{1,0:T(8,128)} %get-tuple-element.66.stats, bf16[1024,1024]{1,0:T(8,128)(2,1)} %get-tuple-element.53.pz_ref, ...), custom_call_target="tpu_custom_call" | custom-call | tf_op jit(solution)/shard_map/gate_norm/pallas_call | solution.py:471
  206.8 100.5 %scan_backward.1 = (bf16[1024,1024]{1,0:T(8,128)(2,1)}, bf16[1024,384]{1,0:T(8,128)(2,1)}, f32[8,1280]{1,0:T(8,128)}, bf16[128,2048]{1,0:T(8,128)(2,1)}, bf16[2,...) custom-call(bf16[1024,1024]{1,0:T(8,128)(2,1)} %get-tuple-element.51.px_ref, ...), custom_call_target="tpu_custom_call" | custom-call | tf_op jit(solution)/shard_map/scan_backward/pallas_call | solution.py:868
  307.4 82.8 %reduce_all.1 = (bf16[4,2,1024,128]{3,2,1,0:T(8,128)(2,1)}, bf16[4,1024,256]{2,1,0:T(8,128)(2,1)}, bf16[4,384,256]{2,1,0:T(8,128)(2,1)}, bf16[4,128,2048]{2,1,0:...) custom-call(bf16[4,2048,256]{2,1,0:T(8,128)(2,1)} %get-tuple-element.71.normed_t, ...), custom_call_target="tpu_custom_call" | custom-call | tf_op jit(solution)/shard_map/reduce_all/pallas_call | solution.py:1592
  390.2 0.8 slice.76
  391.0 0.8 reduce_sum.18
  391.8 0.6 constant_dynamic-slice_fusion.4
  392.4 0.8 slice_reduce_fusion
  393.1 0.9 slice.81
  394.1 0.9 slice.72
  395.1 0.6 constant_dynamic-slice_fusion.2
  395.6 0.1 copy.47
  395.7 0.3 copy.48
  396.0 0.1 reshape.126
  396.2 0.5 slice_bitcast_fusion
  396.8 0.1 fusion
  396.9 0.6 slice_reduce_fusion.1
  397.5 0.6 slice.84
  398.1 4.1 %bitcast_convert_fusion = f32[512,2048]{1,0:T(8,128)} fusion(bf16[4,128,2048]{2,1,0:T(8,128)(2,1)} %get-tuple-element.90), kind=kLoop, calls=%fused_computation | loop fusion | flops 1048576 | bytes 6291456 | tf_op jit(solution)/shard_map/convert_element_type | solution.py:1778
  402.2 8.1 %assemble.1 = f32[8512,256]{1,0:T(8,128)} custom-call(bf16[4,2,1024,128]{3,2,1,0:T(8,128)(2,1)} %get-tuple-element.86.z_ref, bf16[4,1024,256]{2,1,0:T(8,128)(2,1)} %get-tuple-element.87.x_ref, bf16[4,384,256]{2,1,0:T(8,128)(2,1)} %get-tuple-element.88.s_ref), custom_call_target="tpu_custom_call" | custom-call | tf_op jit(solution)/shard_map/assemble/pallas_call | solution.py:1692
  410.3 1.0 copy.62
  411.3 0.6 copy-done.1
  411.9 1.0 copy.63
  (22 shorter events, 0.6 us)
Async XLA Ops:
  402.2 8.1 %copy-start = (bf16[256,2048]{1,0:T(8,128)(2,1)S(1)}, bf16[256,2048]{1,0:T(8,128)(2,1)}, u32[]{:S(2)}) copy-start(bf16[256,2048]{1,0:T(8,128)(2,1)} %get-tuple-element.75) | copy-start | bytes 3145732
  410.3 1.6 copy-start.1
where the time goes:
time: 416 us; the launch traced here: 413 us
  Pallas kernels  385 us (93%)
  local copies, waits for them, and re-layouts  16.4 us (4%)
  other arithmetic  10.2 us (2%)
    pallas_call x1, Pallas kernels, gather_all(): pl.pallas_call(functools.partial(gather_kernel, n, n_ctx, unit, direct),...  143 us
    pallas_call x1, Pallas kernels, scan_backward(): pl.pallas_call(functools.partial(backward_kernel, heads, unit, n_ctx, n),...  101 us
    pallas_call x1, Pallas kernels, reduce_all(): pl.pallas_call(functools.partial(reduce_kernel, n, n_ctx, direct), in_spe...  82.8 us
    pallas_call x1, Pallas kernels, scan_forward(): pl.pallas_call(functools.partial(forward_kernel, heads, unit, n_ctx), gri...  30 us
    pallas_call x1, Pallas kernels, gate_norm(): pl.pallas_call(functools.partial(gate_kernel, width // HEAD, channels), g...  20.7 us

commit v1 on v0

--- a/solution.py
+++ b/solution.py
@@ -66,16 +66,150 @@
     return (at < length_ref[0]).astype(F32)
 
 
+MESH = pl.DeviceIdType.MESH
+SMALL_ROWS = 32
+
+
+def ring_place(index, half):
+    a, b = index // 2, index % 2
+    return a + b * (2 * half - 1 - 2 * a)
+
+
+def ring_index(place, half):
+    b = place // half
+    return 2 * (place + b * (2 * half - 1 - 2 * place)) + b
+
+
+class Ring:
+    def __init__(self, n):
+        self.n, self.half = n, n // 2
+        self.me, self.shard = lax.axis_index("ctx"), lax.axis_index("fsdp")
+        self.place = ring_place(self.shard, self.half)
+
+    def at(self, steps):
+        return ring_index(lax.rem(self.place + steps + 2 * self.n, self.n), self.half)
+
+    def neighbour(self, way):
+        return (self.me, self.at(1 if way == 0 else -1))
+
+
+def remote(source, target, send, recv, device):
+    return pltpu.make_async_remote_copy(
+        src_ref=source,
+        dst_ref=target,
+        send_sem=send,
+        recv_sem=recv,
+        device_id=device,
+        device_id_type=MESH,
+    )
+
+
+def greet(device):
+    pl.semaphore_signal(pltpu.get_barrier_semaphore(), inc=1, device_id=device, device_id_type=MESH)
+
+
+class Around:
+    def __init__(self, me, shard):
+        core, row = me % 2, me // 2
+        self.me = me
+        self.core_at = me + 1 - 2 * core
+        self.row_at = me + 2 - 4 * row
+        self.both_at = self.row_at + 1 - 2 * core
+        self.core, self.row, self.both = (
+            (at, shard) for at in (self.core_at, self.row_at, self.both_at)
+        )
+        self.all = (self.core, self.row, self.both)
+
+
+class TokenSum:
+    def __init__(self, around, parts, own_part, row_part, from_core, from_row, send, recv):
+        self.around, self.parts, self.own_part, self.row_part = around, parts, own_part, row_part
+        self.from_core, self.from_row, self.send, self.recv = from_core, from_row, send, recv
+
+    def loads(self):
+        at = self.around
+        return (
+            (self.parts.at[at.row_at], self.row_part),
+            (self.parts.at[at.me], self.own_part),
+        )
+
+    def to_core(self, which):
+        at = self.around
+        return remote(
+            self.parts.at[(at.core_at, at.both_at)[which]],
+            self.from_core.at[which],
+            self.send.at[which],
+            self.recv.at[which],
+            at.core,
+        )
+
+    def to_row(self):
+        return remote(
+            self.row_part, self.from_row, self.send.at[2], self.recv.at[2], self.around.row
+        )
+
+    def start(self):
+        self.to_core(1).start()
+        self.to_core(0).start()
+
+    def pass_row(self):
+        self.to_core(1).wait()
+        total = self.row_part[...].astype(F32) + self.from_core[1].astype(F32)
+        self.row_part[...] = total.astype(BF16)
+        self.to_row().start()
+
+    def total(self):
+        self.to_core(0).wait()
+        self.to_row().wait()
+        return (
+            self.own_part[...].astype(F32)
+            + self.from_core[0].astype(F32)
+            + self.from_row[...].astype(F32)
+        )
+
+
+class SmallSum:
+    def __init__(self, n, around, whole, sums, send, recv, ctx_send, ctx_recv):
+        self.n, self.around, self.whole, self.sums = n, around, whole, sums
+        self.send, self.recv, self.ctx_send, self.ctx_recv = send, recv, ctx_send, ctx_recv
+        self.shard = lax.axis_index("fsdp")
+
+    def to_peer(self, offset):
+        own = self.whole.at[self.shard]
+        peer = (self.around.me, lax.rem(self.shard + offset, self.n))
+        return remote(own, own, self.send.at[offset - 1], self.recv.at[offset - 1], peer)
+
+    def to_ctx(self, i):
+        own = self.sums.at[self.around.me]
+        return remote(own, own, self.ctx_send.at[i], self.ctx_recv.at[i], self.around.all[i])
+
+    def start(self):
+        lax.fori_loop(1, self.n, lambda j, carry: (self.to_peer(j).start(), carry)[1], 0)
+
+    def add(self):
+        lax.fori_loop(1, self.n, lambda j, carry: (self.to_peer(j).wait(), carry)[1], 0)
+        self.sums[self.around.me] = jnp.sum(self.whole[...], axis=0)
+        for i in range(3):
+            self.to_ctx(i).start()
+
+    def finish(self):
+        for i in range(3):
+            self.to_ctx(i).wait()
+
+
 def forward_kernel(
     heads,
     unit,
     n_ctx,
+    n,
+    direct,
     length_ref,
     px_ref,
     ps_ref,
-    pz_ref,
-    up_ref,
-    w_o,
+    normed_ref,
+    out_weight,
+    w_z,
+    upstream,
     taps_x_ref,
     taps_s_ref,
     gate_gain_ref,
@@ -90,21 +224,117 @@
     step_ref,
     chain_ref,
     kept_ref,
-    y_ref,
-    dyn_ref,
-    stat_ref,
+    gain_ref,
+    gate_t,
+    mixed_parts,
+    d_z,
+    d_ssd,
     state,
     before_x,
     before_s,
     v_o,
+    v_z,
+    v_up,
+    all_y,
+    all_z,
+    all_dyn,
+    v_yt,
+    v_mixed,
+    v_dz,
+    v_dssd,
+    stat_all,
+    columns,
     load_sem,
+    store_sem,
+    ring_send,
+    ring_recv,
+    piece_recv,
+    stat_send,
+    stat_recv,
 ):
     block = pl.program_id(0)
-    load = pltpu.make_async_copy(w_o, v_o, load_sem)
+    blocks = pl.num_programs(0)
+    ring = Ring(n)
+    me, shard = ring.me, ring.shard
+    around = Around(me, shard)
+    width = px_ref.shape[1]
+    channels = width * n_ctx
+    piece, size = v_o.shape[0] // n, v_o.shape[1] // 4
+    points = heads // 2 * n_ctx
+    loads = [
+        pltpu.make_async_copy(source, target, load_sem.at[i])
+        for i, (source, target) in enumerate(((w_z, v_z), (upstream, v_up)))
+    ]
+    shard_rows = lambda index: pl.ds(pl.multiple_of(index * piece, 16), piece)
+    own_piece = out_weight.at[pl.ds(pl.multiple_of(me * piece, 16), piece)]
+    piece_peer = (shard % n_ctx, shard // n_ctx * n_ctx + me)
+    moves = shard % n_ctx != me
+
+    def hop(way, sub, step):
+        at = pl.multiple_of((2 * way + sub) * size, LANES)
+        place = v_o.at[shard_rows(ring.at(step * (2 * way - 1))), pl.ds(at, size)]
+        return remote(
+            place,
+            place,
+            ring_send.at[way, sub],
+            ring_recv.at[way, sub, step],
+            (me, ring.at(1 - 2 * way)),
+        )
+
+    def streams(body):
+        lax.fori_loop(0, 4, lambda e, carry: (body(e // 2, e % 2), carry)[1], 0)
+
+    def ring_step(step):
+        def body(way, sub):
+            hop(way, sub, step).wait()
+
+            @pl.when(step < n - 2)
+            def _():
+                hop(way, sub, step + 1).start()
+
+        streams(body)
+
+    def serve(point):
+        at = block * (heads // 2) + point
+        lax.fori_loop(
+            at * (n - 1) // points,
+            (at + 1) * (n - 1) // points,
+            lambda step, carry: (ring_step(step), carry)[1],
+            0,
+        )
 
     @pl.when(block == 0)
     def _():
-        load.start()
+        for device in around.all:
+            greet(device)
+        greet(ring.neighbour(0))
+        greet(ring.neighbour(1))
+        keep = pltpu.make_async_copy(own_piece, v_o.at[shard_rows(shard)], load_sem.at[2])
+        if direct:
+            keep.start()
+            pl.semaphore_wait(pltpu.get_barrier_semaphore(), 5)
+            keep.wait()
+        else:
+            send = remote(
+                own_piece, v_o.at[shard_rows(piece_peer[1])], load_sem.at[2], piece_recv, piece_peer
+            )
+
+            @pl.when(moves)
+            def _():
+                greet(piece_peer)
+                pl.semaphore_wait(pltpu.get_barrier_semaphore(), 6)
+                send.start()
+                send.wait()
+
+            @pl.when(jnp.logical_not(moves))
+            def _():
+                pl.semaphore_wait(pltpu.get_barrier_semaphore(), 5)
+                keep.start()
+                keep.wait()
+
+        streams(lambda way, sub: hop(way, sub, 0).start())
+        for copy in loads:
+            copy.start()
         state[...] = jnp.zeros_like(state)
         before_x[...] = jnp.zeros_like(before_x)
         before_s[...] = jnp.zeros_like(before_s)
@@ -121,17 +351,14 @@
             total = total + weight[k : k + 1] * padded[first : first + BLOCK]
         return silu_and_slope(total)
 
-    shared = ps_ref[...].astype(F32)
-    both = shared[:, : 2 * STATE]
+    both = ps_ref[:, : 2 * STATE].astype(F32)
     active, slope = conv(both, before_s[...], taps_s_ref[...])
     before_s[...] = both[BLOCK - 8 :]
     slope_s_ref[...] = slope.astype(BF16)
     rows_b, rows_c = active[:, :STATE].astype(BF16), active[:, STATE:].astype(BF16)
     b_ref[...] = rows_b
     c_ref[...] = rows_c
-    chosen = chosen_heads(lax.axis_index("ctx"), heads, unit, n_ctx)
-    raw = mm(ps_ref[:, 2 * STATE :], chosen)
-    raw = raw + head_ref[0:1]
+    raw = mm(ps_ref[:, 2 * STATE :], chosen_heads(me, heads, unit, n_ctx)) + head_ref[0:1]
     own = iota2((1, LANES), 1) < heads
     step = jnp.where(own, valid * jax.nn.softplus(raw), 0.0)
     lam = step * head_ref[1:2]
@@ -144,7 +371,6 @@
     kept_ref[0] = state[...].astype(BF16)
     entering = mm(rows_c, state[...].astype(BF16))
     by_state = rows_b.T
-    squares = jnp.zeros((BLOCK, LANES), F32)
     for first in range(0, heads, 2):
         lanes = slice(first * HEAD, (first + 2) * HEAD)
         current = px_ref[:, lanes].astype(F32)
@@ -159,53 +385,132 @@
         for head, keep in ((first, low_half), (first + 1, jnp.logical_not(low_half))):
             mixing = (gram * spread(level, across, head)).astype(BF16)
             total += mm(mixing, jnp.where(keep, scaled, 0.0).astype(BF16))
-        y_ref[:, lanes] = total
+        all_y[block, :, lanes] = total
         update = mm(by_state, (x * pair_of(weight, first, low_half)).astype(BF16))
         state[:, lanes] = state[:, lanes] * pair_of(last, first, low_half) + update
-        gated = total * jax.nn.silu(pz_ref[:, lanes].astype(F32))
-        squares += gated * gated
+        if first + 2 < heads:
+            serve(first // 2)
 
     @pl.when(block == 0)
     def _():
-        load.wait()
-
-    d_yn = valid * mm(up_ref[0], v_o[...], ((1,), (1,)))
-    dyn_ref[...] = d_yn
-    gated = y_ref[...] * jax.nn.silu(pz_ref[...].astype(F32))
-    terms = gate_gain_ref[...] * d_yn * gated
-    square = jnp.sum(squares, axis=1, keepdims=True)
-    along = jnp.sum(terms, axis=1, keepdims=True)
-    lane = iota2((1, LANES), 1)
-    both_sums = jnp.where(lane == 0, square, 0.0) + jnp.where(lane == 1, along, 0.0)
-    stat_ref[...] = both_sums.T[0:8]
-
-
-def scan_forward(unit, n_ctx, length, px, ps, pz, upstream, w_o, taps_x, taps_s, gate_gain, skip, head):
+        loads[0].wait()
+
+    all_z[block] = mm(normed_ref[...], v_z[...]).astype(BF16)
+    serve(heads // 2 - 1)
+
+    @pl.when(block == blocks - 1)
+    def _():
+        loads[1].wait()
+        lane = iota2((1, LANES), 1)
+
+        def sums_of(chunk, carry):
+            d_yn = column_valid(length_ref, chunk) * mm(v_up[chunk], v_o[...], ((1,), (1,)))
+            all_dyn[chunk] = d_yn
+            gated = all_y[chunk] * jax.nn.silu(all_z[chunk].astype(F32))
+            square = jnp.sum(gated * gated, axis=1, keepdims=True)
+            along = jnp.sum(gate_gain_ref[...] * d_yn * gated, axis=1, keepdims=True)
+            pair = jnp.where(lane == 0, square, 0.0) + jnp.where(lane == 1, along, 0.0)
+            stat_all[me, chunk] = pair.T[0:8]
+            return carry
+
+        lax.fori_loop(0, blocks, sums_of, 0)
+        own_stats = stat_all.at[me]
+        copies = [
+            remote(own_stats, own_stats, stat_send.at[i], stat_recv.at[i], device)
+            for i, device in enumerate(around.all)
+        ]
+        for copy in copies:
+            copy.start()
+        gain_ref[...] = jnp.zeros_like(gain_ref)
+        for copy in copies:
+            copy.wait()
+        total = jnp.sum(stat_all[...], axis=0)
+        for i in range(n_ctx):
+            columns[i] = total[i].T
+
+        def stores(chunk):
+            slot = chunk % 2
+            rows = pl.ds(pl.multiple_of(chunk * BLOCK, BLOCK), BLOCK)
+            return [
+                pltpu.make_async_copy(source.at[slot], target, store_sem.at[slot, i])
+                for i, (source, target) in enumerate(
+                    (
+                        (v_yt, gate_t.at[chunk]),
+                        (v_mixed, mixed_parts.at[chunk]),
+                        (v_dz, d_z.at[rows]),
+                        (v_dssd, d_ssd.at[rows]),
+                    )
+                )
+            ]
+
+        def gate_part(chunk, carry):
+            slot = chunk % 2
+
+            @pl.when(chunk >= 2)
+            def _():
+                for copy in stores(chunk - 2):
+                    copy.wait()
+
+            sums = columns[chunk]
+            scale = lax.rsqrt(sums[:, 0:1] / channels + EPS)
+            slant = scale * scale * scale * sums[:, 1:2] / channels
+            here = column_valid(length_ref, chunk)
+            for first in range(0, heads, 2):
+                lanes = slice(first * HEAD, (first + 2) * HEAD)
+                gate, gate_slope = silu_and_slope(all_z[chunk, :, lanes].astype(F32))
+                mixed = all_y[chunk, :, lanes]
+                d_yn = all_dyn[chunk, :, lanes]
+                gain = gate_gain_ref[:, lanes]
+                gated = mixed * gate
+                scaled = gated * scale
+                all_z[chunk, :, lanes] = (here * (scaled * gain)).astype(BF16)
+                gain_ref[0:1, lanes] += jnp.sum(d_yn * scaled, axis=0, keepdims=True)
+                d_gated = scale * (gain * d_yn) - gated * slant
+                v_dz[slot, :, lanes] = (d_gated * mixed * gate_slope).astype(BF16)
+                v_dssd[slot, :, lanes] = (d_gated * gate).astype(BF16)
+            normed_gate = all_z[chunk]
+            v_yt[slot] = normed_gate.T
+            v_mixed[slot] = mm(normed_gate, v_o[...]).astype(BF16)
+            for copy in stores(chunk):
+                copy.start()
+            return carry
+
+        lax.fori_loop(0, blocks, gate_part, 0)
+        for chunk in (n_ctx - 2, n_ctx - 1):
+            for copy in stores(chunk):
+                copy.wait()
+
+
+def scan_forward(
+    n, direct, unit, n_ctx, length, px, ps, normed, out_weight, w_z, upstream, taps_x, taps_s, gate_gain, skip, head
+):
     tokens, width = px.shape
     heads = width // HEAD
     count = tokens // BLOCK
-    model = w_o.shape[1]
+    model = out_weight.shape[1]
+    assert count == n_ctx
     by_block = lambda i: (i, 0)
     at_block = lambda size: pl.BlockSpec((BLOCK, size), by_block)
     whole = lambda a: pl.BlockSpec(a.shape, lambda i: (0, 0))
+    any_space = pl.BlockSpec(memory_space=pl.ANY)
     low = lambda *shape: jax.ShapeDtypeStruct(shape, BF16)
     full = lambda *shape: jax.ShapeDtypeStruct(shape, F32)
+    v_low = lambda *shape: pltpu.VMEM(shape, BF16)
+    v_full = lambda *shape: pltpu.VMEM(shape, F32)
+    dma = pltpu.SemaphoreType.DMA
     return pl.pallas_call(
-        functools.partial(forward_kernel, heads, unit, n_ctx),
+        functools.partial(forward_kernel, heads, unit, n_ctx, n, direct),
         grid=(count,),
         in_specs=[
             pl.BlockSpec(memory_space=pltpu.SMEM),
             at_block(width),
             at_block(ps.shape[1]),
-            at_block(width),
-            pl.BlockSpec((1, BLOCK, model), lambda i: (i, 0, 0)),
-            pl.BlockSpec(memory_space=pl.ANY),
-            whole(taps_x),
-            whole(taps_s),
-            whole(gate_gain),
-            whole(skip),
-            whole(head),
-        ],
+            at_block(model),
+            any_space,
+            any_space,
+            any_space,
+        ]
+        + [whole(a) for a in (taps_x, taps_s, gate_gain, skip, head)],
         out_specs=[
             at_block(width),
             at_block(STATE),
@@ -216,9 +521,11 @@
             at_block(LANES),
             at_block(LANES),
             pl.BlockSpec((1, STATE, width), lambda i: (i, 0, 0)),
-            at_block(width),
-            at_block(width),
-            pl.BlockSpec((8, BLOCK), lambda i: (0, i)),
+            pl.BlockSpec((8, width), lambda i: (0, 0)),
+            any_space,
+            any_space,
+            any_space,
+            any_space,
         ],
         out_shape=[
             low(tokens, width),
@@ -230,284 +537,47 @@
             full(tokens, LANES),
             full(tokens, LANES),
             low(count, STATE, width),
-            full(tokens, width),
-            full(tokens, width),
-            full(8, tokens),
+            full(8, width),
+            low(count, width, BLOCK),
+            low(count, BLOCK, model),
+            low(tokens, width),
+            low(tokens, width),
         ],
         scratch_shapes=[
-            pltpu.VMEM((STATE, width), F32),
-            pltpu.VMEM((8, width), F32),
-            pltpu.VMEM((8, 2 * STATE), F32),
-            pltpu.VMEM(w_o.shape, BF16),
-            pltpu.SemaphoreType.DMA,
+            v_full(STATE, width),
+            v_full(8, width),
+            v_full(8, 2 * STATE),
+            v_low(width, model),
+            v_low(*w_z.shape),
+            v_low(count, BLOCK, model),
+            v_full(count, BLOCK, width),
+            v_low(count, BLOCK, width),
+            v_full(count, BLOCK, width),
+            v_low(2, width, BLOCK),
+            v_low(2, BLOCK, model),
+            v_low(2, BLOCK, width),
+            v_low(2, BLOCK, width),
+            v_full(n_ctx, count, 8, BLOCK),
+            v_full(count, BLOCK, 8),
+            dma((3,)),
+            dma((2, 4)),
+            dma((2, 2)),
+            dma((2, 2, n - 1)),
+            dma,
+            dma((3,)),
+            dma((3,)),
         ],
-        compiler_params=pltpu.CompilerParams(vmem_limit_bytes=56 * 1024 * 1024),
-        cost_estimate=pl.CostEstimate(
-            flops=2 * tokens * width * (2 * BLOCK + 2 * STATE + model),
-            bytes_accessed=tokens * width * 24,
-            transcendentals=tokens * heads * BLOCK,
+        compiler_params=pltpu.CompilerParams(
+            collective_id=2, has_side_effects=True, vmem_limit_bytes=58 * 1024 * 1024
         ),
         name="scan_forward",
-    )(length, px, ps, pz, upstream, w_o, taps_x, taps_s, gate_gain, skip, head)
+    )(length, px, ps, normed, out_weight, w_z, upstream, taps_x, taps_s, gate_gain, skip, head)
 
 
 def head_sums(product, chooser):
     high = product.astype(BF16)
     rest = (product - high.astype(F32)).astype(BF16)
     return mm(high, chooser) + mm(rest, chooser)
-
-
-MESH = pl.DeviceIdType.MESH
-SMALL_ROWS = 32
-
-
-def ring_place(index, half):
-    a, b = index // 2, index % 2
-    return a + b * (2 * half - 1 - 2 * a)
-
-
-def ring_index(place, half):
-    b = place // half
-    return 2 * (place + b * (2 * half - 1 - 2 * place)) + b
-
-
-class Ring:
-    def __init__(self, n):
-        self.n, self.half = n, n // 2
-        self.me, self.shard = lax.axis_index("ctx"), lax.axis_index("fsdp")
-        self.place = ring_place(self.shard, self.half)
-
-    def at(self, steps):
-        return ring_index(lax.rem(self.place + steps + 2 * self.n, self.n), self.half)
-
-    def neighbour(self, way):
-        return (self.me, self.at(1 if way == 0 else -1))
-
-
-def remote(source, target, send, recv, device):
-    return pltpu.make_async_remote_copy(
-        src_ref=source,
-        dst_ref=target,
-        send_sem=send,
-        recv_sem=recv,
-        device_id=device,
-        device_id_type=MESH,
-    )
-
-
-def greet(device):
-    pl.semaphore_signal(pltpu.get_barrier_semaphore(), inc=1, device_id=device, device_id_type=MESH)
-
-
-class Around:
-    def __init__(self, me, shard):
-        core, row = me % 2, me // 2
-        self.me = me
-        self.core_at = me + 1 - 2 * core
-        self.row_at = me + 2 - 4 * row
-        self.both_at = self.row_at + 1 - 2 * core
-        self.core, self.row, self.both = (
-            (at, shard) for at in (self.core_at, self.row_at, self.both_at)
-        )
-        self.all = (self.core, self.row, self.both)
-
-
-class TokenSum:
-    def __init__(self, around, parts, own_part, row_part, from_core, from_row, send, recv):
-        self.around, self.parts, self.own_part, self.row_part = around, parts, own_part, row_part
-        self.from_core, self.from_row, self.send, self.recv = from_core, from_row, send, recv
-
-    def loads(self):
-        at = self.around
-        return (
-            (self.parts.at[at.row_at], self.row_part),
-            (self.parts.at[at.me], self.own_part),
-        )
-
-    def to_core(self, which):
-        at = self.around
-        return remote(
-            self.parts.at[(at.core_at, at.both_at)[which]],
-            self.from_core.at[which],
-            self.send.at[which],
-            self.recv.at[which],
-            at.core,
-        )
-
-    def to_row(self):
-        return remote(
-            self.row_part, self.from_row, self.send.at[2], self.recv.at[2], self.around.row
-        )
-
-    def start(self):
-        self.to_core(1).start()
-        self.to_core(0).start()
-
-    def pass_row(self):
-        self.to_core(1).wait()
-        total = self.row_part[...].astype(F32) + self.from_core[1].astype(F32)
-        self.row_part[...] = total.astype(BF16)
-        self.to_row().start()
-
-    def total(self):
-        self.to_core(0).wait()
-        self.to_row().wait()
-        return (
-            self.own_part[...].astype(F32)
-            + self.from_core[0].astype(F32)
-            + self.from_row[...].astype(F32)
-        )
-
-
-class SmallSum:
-    def __init__(self, n, around, whole, sums, send, recv, ctx_send, ctx_recv):
-        self.n, self.around, self.whole, self.sums = n, around, whole, sums
-        self.send, self.recv, self.ctx_send, self.ctx_recv = send, recv, ctx_send, ctx_recv
-        self.shard = lax.axis_index("fsdp")
-
-    def to_peer(self, offset):
-        own = self.whole.at[self.shard]
-        peer = (self.around.me, lax.rem(self.shard + offset, self.n))
-        return remote(own, own, self.send.at[offset - 1], self.recv.at[offset - 1], peer)
-
-    def to_ctx(self, i):
-        own = self.sums.at[self.around.me]
-        return remote(own, own, self.ctx_send.at[i], self.ctx_recv.at[i], self.around.all[i])
-
-    def start(self):
-        lax.fori_loop(1, self.n, lambda j, carry: (self.to_peer(j).start(), carry)[1], 0)
-
-    def add(self):
-        lax.fori_loop(1, self.n, lambda j, carry: (self.to_peer(j).wait(), carry)[1], 0)
-        self.sums[self.around.me] = jnp.sum(self.whole[...], axis=0)
-        for i in range(3):
-            self.to_ctx(i).start()
-
-    def finish(self):
-        for i in range(3):
-            self.to_ctx(i).wait()
-
-
-def gate_kernel(
-    heads,
-    channels,
-    length_ref,
-    stats,
-    pz_ref,
-    y_ref,
-    dyn_ref,
-    w_o,
-    gate_gain_ref,
-    ynt_ref,
-    mixed_ref,
-    dz_ref,
-    dssd_ref,
-    gain_ref,
-    stat_all,
-    columns,
-    v_y,
-    v_o,
-    load_sem,
-    stat_send,
-    stat_recv,
-):
-    block = pl.program_id(0)
-    me = lax.axis_index("ctx")
-    around = Around(me, lax.axis_index("fsdp"))
-    load = pltpu.make_async_copy(w_o, v_o, load_sem.at[0])
-
-    @pl.when(block == 0)
-    def _():
-        for device in around.all:
-            greet(device)
-        load.start()
-        own = pltpu.make_async_copy(stats, stat_all.at[me], load_sem.at[1])
-        own.start()
-        own.wait()
-        pl.semaphore_wait(pltpu.get_barrier_semaphore(), 3)
-        copies = [
-            remote(stat_all.at[me], stat_all.at[me], stat_send.at[i], stat_recv.at[i], device)
-            for i, device in enumerate(around.all)
-        ]
-        for copy in copies:
-            copy.start()
-        for copy in copies:
-            copy.wait()
-        total = jnp.sum(stat_all[...], axis=0)
-        for i in range(total.shape[1] // BLOCK):
-            columns[i] = total[:, i * BLOCK : (i + 1) * BLOCK].T
-        gain_ref[...] = jnp.zeros_like(gain_ref)
-        load.wait()
-
-    valid = column_valid(length_ref, block)
-    sums = columns[block]
-    scale = lax.rsqrt(sums[:, 0:1] / channels + EPS)
-    slant = scale * scale * scale * sums[:, 1:2] / channels
-    for first in range(0, heads, 2):
-        lanes = slice(first * HEAD, (first + 2) * HEAD)
-        gate, gate_slope = silu_and_slope(pz_ref[:, lanes].astype(F32))
-        mixed = y_ref[:, lanes]
-        d_yn = dyn_ref[:, lanes]
-        gain = gate_gain_ref[:, lanes]
-        gated = mixed * gate
-        scaled = gated * scale
-        v_y[:, lanes] = (valid * (scaled * gain)).astype(BF16)
-        gain_ref[0:1, lanes] += jnp.sum(d_yn * scaled, axis=0, keepdims=True)
-        d_gated = scale * (gain * d_yn) - gated * slant
-        dz_ref[:, lanes] = (d_gated * mixed * gate_slope).astype(BF16)
-        dssd_ref[:, lanes] = (d_gated * gate).astype(BF16)
-    normed_gate = v_y[...]
-    ynt_ref[...] = normed_gate.T
-    mixed_ref[0] = mm(normed_gate, v_o[...]).astype(BF16)
-
-
-def gate_norm(channels, length, stats, pz, y, d_yn, w_o, gate_gain):
-    tokens, width = pz.shape
-    count, model = tokens // BLOCK, w_o.shape[1]
-    n_ctx = channels // width
-    at_block = lambda size: pl.BlockSpec((BLOCK, size), lambda i: (i, 0))
-    any_space = pl.BlockSpec(memory_space=pl.ANY)
-    low = lambda *shape: jax.ShapeDtypeStruct(shape, BF16)
-    return pl.pallas_call(
-        functools.partial(gate_kernel, width // HEAD, channels),
-        grid=(count,),
-        in_specs=[
-            pl.BlockSpec(memory_space=pltpu.SMEM),
-            any_space,
-            at_block(width),
-            at_block(width),
-            at_block(width),
-            any_space,
-            pl.BlockSpec(gate_gain.shape, lambda i: (0, 0)),
-        ],
-        out_specs=[
-            pl.BlockSpec((width, BLOCK), lambda i: (0, i)),
-            pl.BlockSpec((1, BLOCK, model), lambda i: (i, 0, 0)),
-            at_block(width),
-            at_block(width),
-            pl.BlockSpec((8, width), lambda i: (0, 0)),
-        ],
-        out_shape=[
-            low(width, tokens),
-            low(count, BLOCK, model),
-            low(tokens, width),
-            low(tokens, width),
-            jax.ShapeDtypeStruct((8, width), F32),
-        ],
-        scratch_shapes=[
-            pltpu.VMEM((n_ctx, 8, tokens), F32),
-            pltpu.VMEM((count, BLOCK, 8), F32),
-            pltpu.VMEM((BLOCK, width), BF16),
-            pltpu.VMEM(w_o.shape, BF16),
-            pltpu.SemaphoreType.DMA((2,)),
-            pltpu.SemaphoreType.DMA((3,)),
-            pltpu.SemaphoreType.DMA((3,)),
-        ],
-        compiler_params=pltpu.CompilerParams(
-            collective_id=2, has_side_effects=True, vmem_limit_bytes=56 * 1024 * 1024
-        ),
-        name="gate_norm",
-    )(length, stats, pz, y, d_yn, w_o, gate_gain)
 
 
 def backward_kernel(
@@ -586,7 +656,7 @@
         pltpu.make_async_copy(source, target, load_sem.at[i])
         for i, (source, target) in enumerate(
             (
-                (gate_t, v_left.at[pl.ds(0, width)]),
+                *((gate_t.at[c], v_left.at[pl.ds(0, width), pl.ds(c * own, own)]) for c in range(n_ctx)),
                 *((upstream.at[c], v_right.at[pl.ds(c * own, own), pl.ds(0, model)]) for c in range(n_ctx)),
                 *((normed_t.at[c], v_left.at[pl.ds(width, model), pl.ds(c * own, own)]) for c in range(n_ctx)),
                 (d_z, v_right.at[:, pl.ds(model, width)]),
@@ -595,7 +665,7 @@
             )
         )
     ]
-    ring_loads = 2 + 2 * n_ctx
+    ring_loads = 1 + 3 * n_ctx
 
     def partial_sum(kind, way, sub, index):
         first = (1 - kind) * index * piece + kind * (width + (2 * index + way) * piece)
@@ -921,7 +991,7 @@
             v_low(2, own, model),
             v_low(own, model),
             v_low(own, model),
-            dma((5 + 2 * n_ctx,)),
+            dma((4 + 3 * n_ctx,)),
             dma((3,)),
             dma((2, 2, 2)),
             dma((2, 2, 2, n - 1)),
@@ -941,46 +1011,41 @@
     n,
     n_ctx,
     unit,
-    direct,
     hidden,
     cotangent,
     in_weight_t,
     small,
-    out_weight,
     cotangent_all,
     w_x,
     w_s,
     w_z,
-    w_o,
     small_out,
     proj_x,
     proj_s,
-    proj_z,
+    normed_out,
     normed_t,
     v_hidden,
     v_normed,
     v_x,
     v_s,
-    v_z,
+    own_z,
     v_small,
     raw_x,
     raw_s,
     raw_z,
     out_x,
     out_s,
-    out_z,
     out_t,
     v_gain,
     load_sem,
     column_sem,
     local_sem,
+    keep_sem,
     store_sem,
     ring_send,
     ring_recv,
     ctx_send,
     ctx_recv,
-    piece_send,
-    piece_recv,
 ):
     ring = Ring(n)
     me, shard = ring.me, ring.shard
@@ -991,10 +1056,6 @@
     row = me // 2
     other_core = (me + 1 - 2 * (me % 2), shard)
     other_row = (me + 2 - 4 * row, shard)
-    piece = w_o.shape[1]
-    piece_peer = (shard % n_ctx, shard // n_ctx * n_ctx + me)
-    moves = shard % n_ctx != me
-
     barrier = pltpu.get_barrier_semaphore()
     for device in (other_core, other_row, ring.neighbour(0), ring.neighbour(1)):
         pl.semaphore_signal(barrier, inc=1, device_id=device, device_id_type=MESH)
@@ -1030,32 +1091,17 @@
         for copy in loads[i]:
             copy.wait()
 
-    if direct:
-        pl.semaphore_wait(barrier, 4)
-    else:
-
-        @pl.when(moves)
-        def _():
-            pl.semaphore_signal(barrier, inc=1, device_id=piece_peer, device_id_type=MESH)
-            pl.semaphore_wait(barrier, 5)
-
-        @pl.when(jnp.logical_not(moves))
-        def _():
-            pl.semaphore_wait(barrier, 4)
-
-    half, quarter = width // 2, w_o.shape[2] // 4
+    pl.semaphore_wait(barrier, 4)
+
+    half = width // 2
     rows = r // 2
     both_rows = lambda index, way: pl.ds(pl.multiple_of((2 * index + way) * rows, 16), rows)
     x_part = lambda a, sub: lambda index, way: a.at[both_rows(index, way), pl.ds(sub * half, half)]
     s_part = lambda index, way: v_s.at[both_rows(index, way)]
     small_part = lambda index, way: v_small.at[index, pl.ds(way * SMALL_ROWS // 2, SMALL_ROWS // 2)]
-    o_part = lambda sub: lambda index, way: w_o.at[
-        index, :, pl.ds((2 * way + sub) * quarter, quarter)
-    ]
     phases = (
         ((0, small_part), (1, s_part), (2, x_part(v_x, 0)), (3, x_part(v_x, 1))),
-        ((4, x_part(v_z, 0)), (5, x_part(v_z, 1))),
-        ((6, o_part(0)), (7, o_part(1))),
+        ((4, x_part(w_z, 0)), (5, x_part(w_z, 1))),
     )
 
     def hop(stream, way, step):
@@ -1101,28 +1147,14 @@
     raw_s[shared:, :] = jnp.zeros((raw_s.shape[0] - shared, r), BF16)
     v_s[own_rows, :] = raw_s[...].T
     start_stream(phases[0][1])
-    own_piece = out_weight.at[pl.ds(pl.multiple_of(me * piece, 16), piece)]
-    keep_piece = pltpu.make_async_copy(own_piece, w_o.at[shard], piece_send)
-
-    def move_piece(wait):
-        if direct:
-            keep_piece.wait() if wait else keep_piece.start()
-            return
-        send_piece = remote(own_piece, w_o.at[piece_peer[1]], piece_send, piece_recv, piece_peer)
-
-        @pl.when(moves)
-        def _():
-            send_piece.wait() if wait else send_piece.start()
-
-        @pl.when(jnp.logical_not(moves))
-        def _():
-            keep_piece.wait() if wait else keep_piece.start()
-
     keep_cotangent = pltpu.make_async_copy(cotangent, cotangent_all.at[me], local_sem)
     keep_cotangent.start()
     loaded(3)
     loaded(4)
-    v_z[own_rows, :] = raw_z[...].T
+    own_z[...] = raw_z[...].T
+    keep_z = pltpu.make_async_copy(own_z, w_z.at[own_rows], keep_sem)
+    keep_z.start()
+    keep_z.wait()
 
     def run_phase(number, work, after):
         def body(step, carry):
@@ -1156,11 +1188,6 @@
         v_normed[at, :] = normed
         out_x[at, :] = mm(normed, v_x[...]).astype(BF16)
         out_s[at, :] = mm(normed, v_s[...]).astype(BF16)
-
-    def project_gate(chunk):
-        at = pl.ds(pl.multiple_of(chunk * tokens, tokens), tokens)
-        normed = v_normed[at, :]
-        out_z[at, :] = mm(normed, v_z[...]).astype(BF16)
         out_t[chunk] = normed.T
 
     stores = [
@@ -1172,8 +1199,7 @@
                 (v_small, small_out),
                 (out_x, proj_x),
                 (out_s, proj_s),
-                (v_z, w_z),
-                (out_z, proj_z),
+                (v_normed, normed_out),
                 (out_t, normed_t),
             )
         )
@@ -1184,7 +1210,6 @@
             start_stream(stream)
         to_row(0, hidden, v_hidden).wait_recv()
         pass_on(0, v_hidden).start()
-        move_piece(False)
         to_row(1, cotangent, cotangent_all).start()
         to_core(1, cotangent, cotangent_all).start()
         to_row(0, hidden, v_hidden).wait_send()
@@ -1192,17 +1217,10 @@
         pass_on(0, v_hidden).wait()
 
     def after_second():
-        move_piece(True)
-        for stream in phases[2]:
-            start_stream(stream)
         to_row(1, cotangent, cotangent_all).wait_recv()
         pass_on(1, cotangent_all).start()
-
-    def after_third():
-        to_row(1, cotangent, cotangent_all).wait_send()
-        to_core(1, cotangent, cotangent_all).wait()
-        pass_on(1, cotangent_all).wait()
-        keep_cotangent.wait()
+        for copy in stores[3:]:
+            copy.start()
 
     run_phase(0, None, after_first)
     for f in range(n):
@@ -1210,38 +1228,35 @@
     for copy in stores[0:3]:
         copy.start()
     run_phase(1, project_first, after_second)
-    for copy in stores[3:6]:
-        copy.start()
-    run_phase(2, project_gate, after_third)
-    for copy in stores[6:]:
-        copy.start()
+    to_row(1, cotangent, cotangent_all).wait_send()
+    to_core(1, cotangent, cotangent_all).wait()
+    pass_on(1, cotangent_all).wait()
+    keep_cotangent.wait()
     for copy in stores:
         copy.wait()
 
 
-def gather_all(n, n_ctx, unit, direct, hidden, cotangent, in_weight_t, small, out_weight, shared_width):
+def gather_all(n, n_ctx, unit, width, hidden, cotangent, in_weight_t, small, shared_width):
     own, model = hidden.shape
     tokens = own * n_ctx
-    width = out_weight.shape[0] * n // n_ctx
     rows = in_weight_t.shape[1]
     any_space = pl.BlockSpec(memory_space=pl.ANY)
     low = lambda *shape: jax.ShapeDtypeStruct(shape, BF16)
     v_low = lambda *shape: pltpu.VMEM(shape, BF16)
     dma = pltpu.SemaphoreType.DMA
     return pl.pallas_call(
-        functools.partial(gather_kernel, n, n_ctx, unit, direct),
-        in_specs=[any_space] * 5,
-        out_specs=[any_space] * 10,
+        functools.partial(gather_kernel, n, n_ctx, unit),
+        in_specs=[any_space] * 4,
+        out_specs=[any_space] * 9,
         out_shape=[
             low(n_ctx, own, model),
             low(model, width),
             low(model, shared_width),
             low(model, width),
-            low(n, width // n, model),
             low(n, small.shape[0], small.shape[1]),
             low(tokens, width),
             low(tokens, shared_width),
-            low(tokens, width),
+            low(tokens, model),
             low(n_ctx, model, own),
         ],
         scratch_shapes=[
@@ -1249,32 +1264,30 @@
             v_low(tokens, model),
             v_low(model, width),
             v_low(model, shared_width),
-            v_low(model, width),
+            v_low(rows, width),
             v_low(n, small.shape[0], small.shape[1]),
             v_low(width, rows),
             v_low(shared_width, rows),
             v_low(width, rows),
             v_low(tokens, width),
             v_low(tokens, shared_width),
-            v_low(tokens, width),
             v_low(n_ctx, model, own),
             pltpu.VMEM((1, model), F32),
             dma((3,)),
             dma((2, width // (unit * HEAD))),
             dma,
-            dma((8,)),
-            dma((8, 2)),
-            dma((8, 2, n - 1)),
+            dma,
+            dma((7,)),
+            dma((6, 2)),
+            dma((6, 2, n - 1)),
             dma((2, 3)),
             dma((2, 3)),
-            dma,
-            dma,
         ],
         compiler_params=pltpu.CompilerParams(
             collective_id=0, has_side_effects=True, vmem_limit_bytes=56 * 1024 * 1024
         ),
         name="gather_all",
-    )(hidden, cotangent, in_weight_t, small, out_weight)
+    )(hidden, cotangent, in_weight_t, small)
 
 
 def reduce_kernel(
@@ -1740,10 +1753,9 @@
     longest = -(-max(a.shape[1] for a in lines) // LANES) * LANES
     small = jnp.concatenate([jnp.pad(a, ((0, 0), (0, longest - a.shape[1]))) for a in lines])
     small = jnp.pad(small, ((0, SMALL_ROWS - small.shape[0]), (0, 0)))
-    upstream, w_x, w_s, w_z, w_o, small_all, proj_x, proj_s, proj_z, normed_t = gather_all(
-        n_fsdp, n_ctx, unit, direct, hidden[0], cotangent[0], in_weight.T, small, out_weight, shared_width
+    upstream, w_x, w_s, w_z, small_all, proj_x, proj_s, normed, normed_t = gather_all(
+        n_fsdp, n_ctx, unit, width, hidden[0], cotangent[0], in_weight.T, small, shared_width
     )
-    w_o = w_o.reshape(-1, model)
 
     def line(first, count, size):
         rows = small_all[:, first : first + count, :size]
@@ -1762,11 +1774,8 @@
     head = jnp.pad(jnp.stack([each[0], jnp.exp(each[1])]), ((0, 0), (0, LANES - heads)))
     skip = jnp.repeat(each[2], HEAD)[None]
 
-    *kept_parts, y, d_yn, stats = scan_forward(
-        unit, n_ctx, seq_lens, proj_x, proj_s, proj_z, upstream, w_o, taps_x, taps_s, gain_gate, skip, head
-    )
-    gate_t, mixed_parts, d_z, d_ssd, gain_grads = gate_norm(
-        inner, seq_lens, stats, proj_z, y, d_yn, w_o, gain_gate
+    *kept_parts, gain_grads, gate_t, mixed_parts, d_z, d_ssd = scan_forward(
+        n_fsdp, direct, unit, n_ctx, seq_lens, proj_x, proj_s, normed, out_weight, w_z, upstream, taps_x, taps_s, gain_gate, skip, head
     )
     d_x, d_s, small_grads, shard_o, shard_z, layer_out = scan_backward(
         n_fsdp, unit, n_ctx, proj_x, proj_s, kept_parts, d_ssd, gate_t, normed_t, upstream, d_z, mixed_parts, hidden[0], gain_grads, taps_x, taps_s, skip, head

time: 416 us -> 401 us (0.964)
  Pallas kernels: 385 us -> 366 us
    pallas_call x3 -> x2, Pallas kernels: 193 us -> 174 us  [the longest x1 102 us: gather_all(): pl.pallas_call(functools.partial(gather_kernel, n, n_ctx, unit), in_specs...]
where the time goes in v1:
time: 401 us; the launch traced here: 395 us
  Pallas kernels  366 us (91%)
  local copies, waits for them, and re-layouts  16.4 us (4%)
  other arithmetic  10.2 us (3%)
    pallas_call x1, Pallas kernels, gather_all(): pl.pallas_call(functools.partial(gather_kernel, n, n_ctx, unit), in_specs...  102 us
    pallas_call x1, Pallas kernels, scan_backward(): pl.pallas_call(functools.partial(backward_kernel, heads, unit, n_ctx, n),...  101 us
    pallas_call x1, Pallas kernels, reduce_all(): pl.pallas_call(functools.partial(reduce_kernel, n, n_ctx, direct), in_spe...  83.4 us
    pallas_call x1, Pallas kernels, scan_forward(): pl.pallas_call(functools.partial(forward_kernel, heads, unit, n_ctx, n, d...  72.5 us
    pallas_call x1, Pallas kernels, assemble(): pl.pallas_call(functools.partial(assemble_kernel, part), grid=(2 * n_ctx...  8.09 us

profile of v1, /device:TPU:17, one launch (start us, length us, event | category | flops | bytes accessed | tf_op | source)
XLA Modules:
  0.0 395.0 jit_solution(18002644157557028428)
XLA Ops:
  1.3 0.8 maximum_bitcast_fusion
  2.1 0.7 broadcast_in_dim.21
  2.7 0.7 broadcast_in_dim.23
  3.4 0.7 broadcast_in_dim.22
  4.1 0.7 pad.29
  4.9 0.6 pad.33.small
  5.5 101.7 %gather_all.1 = (bf16[4,256,2048]{2,1,0:T(8,128)(2,1)}, bf16[2048,1024]{1,0:T(8,128)(2,1)}, bf16[2048,384]{1,0:T(8,128)(2,1)}, bf16[2048,1024]{1,0:T(8,128)(2,1)...) custom-call(bf16[256,2048]{1,0:T(8,128)(2,1)} %bitcast.62, ...), custom_call_target="tpu_custom_call" | custom-call | tf_op jit(solution)/shard_map/gather_all/pallas_call | solution.py:1247
  107.2 0.7 convert_reduce_fusion
  108.0 0.8 slice.71
  108.7 0.6 convert.8.gain
  109.3 0.1 reshape.130
  109.4 0.1 copy.40
  109.5 0.1 copy.42
  109.6 0.1 slice.69
  109.7 0.1 copy.41
  109.7 0.1 squeeze.39
  109.8 0.1 copy.43
  109.9 0.1 exp.14
  110.0 0.6 select_maximum_fusion.head_ref
  110.7 0.7 broadcast_in_dim_reshape.3.skip_ref
  111.3 0.9 slice_convert_fusion
  112.2 0.9 convert_bitcast_fusion
  113.1 0.6 dynamic-slice_bitcast_fusion.gate_gain_ref
  113.7 0.1 reshape.125
  113.8 0.6 slice.83.taps_s_ref
  114.6 0.6 copy.57
  115.2 72.5 %scan_forward.1 = (bf16[1024,1024]{1,0:T(8,128)(2,1)}, bf16[1024,128]{1,0:T(8,128)(2,1)}, bf16[1024,128]{1,0:T(8,128)(2,1)}, bf16[1024,1024]{1,0:T(8,128)(2,1)},...) custom-call(s32[1]{0:T(128)S(6)} %copy.61.length_ref, ...), custom_call_target="tpu_custom_call" | custom-call | tf_op jit(solution)/shard_map/scan_forward/pallas_call | solution.py:501
  187.7 100.8 %scan_backward.1 = (bf16[1024,1024]{1,0:T(8,128)(2,1)}, bf16[1024,384]{1,0:T(8,128)(2,1)}, f32[8,1280]{1,0:T(8,128)}, bf16[128,2048]{1,0:T(8,128)(2,1)}, bf16[2,...) custom-call(bf16[1024,1024]{1,0:T(8,128)(2,1)} %get-tuple-element.47.px_ref, ...), custom_call_target="tpu_custom_call" | custom-call | tf_op jit(solution)/shard_map/scan_backward/pallas_call | solution.py:938
  288.5 83.4 %reduce_all.1 = (bf16[4,2,1024,128]{3,2,1,0:T(8,128)(2,1)}, bf16[4,1024,256]{2,1,0:T(8,128)(2,1)}, bf16[4,384,256]{2,1,0:T(8,128)(2,1)}, bf16[4,128,2048]{2,1,0:...) custom-call(bf16[4,2048,256]{2,1,0:T(8,128)(2,1)} %get-tuple-element.64.normed_t, ...), custom_call_target="tpu_custom_call" | custom-call | tf_op jit(solution)/shard_map/reduce_all/pallas_call | solution.py:1605
  371.9 0.8 slice.76
  372.7 0.8 reduce_sum.18
  373.5 0.6 constant_dynamic-slice_fusion.4
  374.1 0.8 slice_reduce_fusion
  374.8 0.9 slice.81
  375.8 0.9 slice.72
  376.8 0.6 constant_dynamic-slice_fusion.2
  377.3 0.1 copy.47
  377.4 0.3 copy.48
  377.7 0.1 reshape.122
  377.9 0.5 slice_bitcast_fusion
  378.5 0.1 fusion
  378.6 0.6 slice_reduce_fusion.1
  379.2 0.6 slice.84
  379.8 4.1 %bitcast_convert_fusion = f32[512,2048]{1,0:T(8,128)} fusion(bf16[4,128,2048]{2,1,0:T(8,128)(2,1)} %get-tuple-element.82), kind=kLoop, calls=%fused_computation | loop fusion | flops 1048576 | bytes 6291456 | tf_op jit(solution)/shard_map/convert_element_type | solution.py:1787
  383.9 8.1 %assemble.1 = f32[8512,256]{1,0:T(8,128)} custom-call(bf16[4,2,1024,128]{3,2,1,0:T(8,128)(2,1)} %get-tuple-element.78.z_ref, bf16[4,1024,256]{2,1,0:T(8,128)(2,1)} %get-tuple-element.79.x_ref, bf16[4,384,256]{2,1,0:T(8,128)(2,1)} %get-tuple-element.80.s_ref), custom_call_target="tpu_custom_call" | custom-call | tf_op jit(solution)/shard_map/assemble/pallas_call | solution.py:1705
  392.0 1.0 copy.62
  393.0 0.6 copy-done.1
  393.6 1.0 copy.63
  (21 shorter events, 0.5 us)
Async XLA Ops:
  383.9 8.1 %copy-start = (bf16[256,2048]{1,0:T(8,128)(2,1)S(1)}, bf16[256,2048]{1,0:T(8,128)(2,1)}, u32[]{:S(2)}) copy-start(bf16[256,2048]{1,0:T(8,128)(2,1)} %get-tuple-element.68) | copy-start | bytes 3145732
  392.0 1.6 copy-start.1

commit v2 on v1

--- a/solution.py
+++ b/solution.py
@@ -59,6 +59,29 @@
         here, there = there, here
     head = (here // unit * n_ctx + me) * unit + here % unit
     return jnp.where(jnp.logical_and(there == head, here < heads), 1.0, 0.0).astype(BF16)
+
+
+class Lines:
+    def __init__(self, ref, first, rows, at, size):
+        self.ref, self.first, self.at, self.shape = ref, first, at, (rows, size)
+
+    def __getitem__(self, index):
+        rows = slice(self.first, self.first + self.shape[0])
+        lanes = slice(0, self.shape[1]) if index is Ellipsis else index[1]
+        return self.ref[rows, self.at + lanes.start : self.at + lanes.stop]
+
+
+def parameters(par_ref, width):
+    lines = par_ref.shape[0] - 3
+    head = par_ref[lines + 2 : lines + 3, 0 : 2 * LANES]
+    return (
+        Lines(par_ref, 0, lines, 0, width),
+        Lines(par_ref, 0, lines, width, 2 * STATE),
+        Lines(par_ref, lines, 1, 0, width),
+        Lines(par_ref, lines + 1, 1, 0, width),
+        head[:, :LANES],
+        head[:, LANES:],
+    )
 
 
 def column_valid(length_ref, block):
@@ -210,11 +233,7 @@
     out_weight,
     w_z,
     upstream,
-    taps_x_ref,
-    taps_s_ref,
-    gate_gain_ref,
-    skip_ref,
-    head_ref,
+    par_ref,
     x_ref,
     b_ref,
     c_ref,
@@ -258,6 +277,7 @@
     me, shard = ring.me, ring.shard
     around = Around(me, shard)
     width = px_ref.shape[1]
+    taps_x_ref, taps_s_ref, gate_gain_ref, skip_ref, bias_step, rate = parameters(par_ref, width)
     channels = width * n_ctx
     piece, size = v_o.shape[0] // n, v_o.shape[1] // 4
     points = heads // 2 * n_ctx
@@ -351,17 +371,17 @@
             total = total + weight[k : k + 1] * padded[first : first + BLOCK]
         return silu_and_slope(total)
 
-    both = ps_ref[:, : 2 * STATE].astype(F32)
+    both = jnp.concatenate([ps_ref[0], ps_ref[1]], axis=1).astype(F32)
     active, slope = conv(both, before_s[...], taps_s_ref[...])
     before_s[...] = both[BLOCK - 8 :]
     slope_s_ref[...] = slope.astype(BF16)
     rows_b, rows_c = active[:, :STATE].astype(BF16), active[:, STATE:].astype(BF16)
     b_ref[...] = rows_b
     c_ref[...] = rows_c
-    raw = mm(ps_ref[:, 2 * STATE :], chosen_heads(me, heads, unit, n_ctx)) + head_ref[0:1]
+    raw = mm(ps_ref[2], chosen_heads(me, heads, unit, n_ctx)) + bias_step
     own = iota2((1, LANES), 1) < heads
     step = jnp.where(own, valid * jax.nn.softplus(raw), 0.0)
-    lam = step * head_ref[1:2]
+    lam = step * rate
     step_ref[...] = step
     lam_ref[...] = lam
     chain_ref[...] = jnp.where(own, valid * jax.nn.sigmoid(raw), 0.0)
@@ -482,7 +502,7 @@
 
 
 def scan_forward(
-    n, direct, unit, n_ctx, length, px, ps, normed, out_weight, w_z, upstream, taps_x, taps_s, gate_gain, skip, head
+    n, direct, unit, n_ctx, length, px, ps, normed, out_weight, w_z, upstream, par
 ):
     tokens, width = px.shape
     heads = width // HEAD
@@ -504,13 +524,13 @@
         in_specs=[
             pl.BlockSpec(memory_space=pltpu.SMEM),
             at_block(width),
-            at_block(ps.shape[1]),
+            pl.BlockSpec((n_ctx, BLOCK, LANES), lambda i: (0, i, 0)),
             at_block(model),
             any_space,
             any_space,
             any_space,
         ]
-        + [whole(a) for a in (taps_x, taps_s, gate_gain, skip, head)],
+        + [whole(par)],
         out_specs=[
             at_block(width),
             at_block(STATE),
@@ -571,7 +591,7 @@
             collective_id=2, has_side_effects=True, vmem_limit_bytes=58 * 1024 * 1024
         ),
         name="scan_forward",
-    )(length, px, ps, normed, out_weight, w_z, upstream, taps_x, taps_s, gate_gain, skip, head)
+    )(length, px, ps, normed, out_weight, w_z, upstream, par)
 
 
 def head_sums(product, chooser):
@@ -604,13 +624,10 @@
     mixed_parts,
     hidden,
     gain_grads_ref,
-    taps_x_ref,
-    taps_s_ref,
-    skip_ref,
-    head_ref,
+    par_ref,
     dx_ref,
-    ds_ref,
     small_ref,
+    d_s,
     shard_o,
     shard_z,
     layer_out,
@@ -633,6 +650,9 @@
     mine,
     from_core,
     from_row,
+    shared_parts,
+    shared_core,
+    shared_row,
     v_hidden,
     load_sem,
     store_sem,
@@ -640,17 +660,30 @@
     ring_recv,
     part_send,
     part_recv,
+    shared_send,
+    shared_recv,
 ):
     turn = pl.program_id(0)
     turns = heads // 2 // POINTS
     block = pl.num_programs(0) - 1 - turn
     width, model = x_ref.shape[1], v_hidden.shape[1]
+    taps_x_ref, taps_s_ref, _, skip_ref, _, rate = parameters(par_ref, width)
     own = hidden.shape[0]
     ring = Ring(n)
     around = Around(ring.me, ring.shard)
     piece, size = slots.shape[4], slots.shape[5]
     sum_mixed = TokenSum(
         around, mixed_parts, mine.at[0], mine.at[1], from_core, from_row, part_send, part_recv
+    )
+    sum_shared = TokenSum(
+        around,
+        shared_parts,
+        shared_parts.at[ring.me],
+        shared_parts.at[around.row_at],
+        shared_core,
+        shared_row,
+        shared_send,
+        shared_recv,
     )
     loads = [
         pltpu.make_async_copy(source, target, load_sem.at[i])
@@ -766,6 +799,8 @@
         greet(ring.neighbour(1))
         for copy in loads:
             copy.start()
+        for c in range(3, n_ctx):
+            shared_parts[c] = jnp.zeros(shared_parts.shape[1:], BF16)
         back[...] = jnp.zeros_like(back)
         small_ref[...] = jnp.zeros_like(small_ref)
         small_ref[taps_x_ref.shape[0] : taps_x_ref.shape[0] + 1, 0:width] = gain_grads_ref[0:1, :]
@@ -870,12 +905,15 @@
     all_pairs = mixed_grads[...]
     d_b = d_b + mm(all_pairs.T.astype(BF16), rows_c)
     d_c = d_c + mm(all_pairs.astype(BF16), rows_b)
+    both = jnp.concatenate([ps_ref[0], ps_ref[1]], axis=1).astype(F32)
     d_conv = jnp.concatenate([d_b, d_c], axis=1) * slope_s_ref[...].astype(F32)
     d_in, grads = conv_back(
-        d_conv, after_s[...], ps_ref[:, : 2 * STATE].astype(F32), taps_s_ref[...]
+        d_conv, after_s[...], both, taps_s_ref[...]
     )
     after_s[...] = d_conv[0:8]
-    ds_ref[:, : 2 * STATE] = d_in.astype(BF16)
+    here = pl.ds(pl.multiple_of(block * BLOCK, BLOCK), BLOCK)
+    shared_parts[0, here, :] = d_in[:, :STATE].astype(BF16)
+    shared_parts[1, here, :] = d_in[:, STATE:].astype(BF16)
     small_ref[0 : taps + 1, width:] += grads
 
     chooser = (iota2((width, LANES), 0) // HEAD == iota2((width, LANES), 1)).astype(BF16)
@@ -886,7 +924,7 @@
     final = -total[0:1, :] - last * total[1:2, :]
     d_level = d_level + jnp.where(iota2((BLOCK, 1), 0) == BLOCK - 1, final, 0.0)
     d_lam = mm_exact((at_row <= at_col).astype(F32), d_level)
-    d_raw = (d_step + d_lam * head_ref[1:2]) * chain_ref[...]
+    d_raw = (d_step + d_lam * rate) * chain_ref[...]
     head_row = taps + 2
     small_ref[head_row : head_row + 1, 0:LANES] += jnp.sum(d_raw, axis=0, keepdims=True)
     small_ref[head_row : head_row + 1, LANES : 2 * LANES] += jnp.sum(
@@ -894,7 +932,13 @@
     )
     small_ref[head_row : head_row + 1, 2 * LANES : 3 * LANES] += total[2:3, :]
     chosen = chosen_heads(lax.axis_index("ctx"), heads, unit, n_ctx, True)
-    ds_ref[:, 2 * STATE :] = mm(d_raw.astype(BF16), chosen).astype(BF16)
+    shared_parts[2, here, :] = mm(d_raw.astype(BF16), chosen).astype(BF16)
+
+    @pl.when(turn == pl.num_programs(0) - 1)
+    def _():
+        sum_shared.start()
+        sum_shared.pass_row()
+
 
     serve(POINTS - 1)
 
@@ -903,26 +947,32 @@
         stores = [
             pltpu.make_async_copy(source, target, store_sem.at[i])
             for i, (source, target) in enumerate(
-                ((done_o, shard_o), (done_z, shard_z), (v_hidden, layer_out))
+                (
+                    (done_o, shard_o),
+                    (done_z, shard_z),
+                    (v_hidden, layer_out),
+                    (shared_parts.at[ring.me], d_s),
+                )
             )
         ]
         stores[0].start()
         stores[1].start()
         v_hidden[...] = (v_hidden[...].astype(F32) + sum_mixed.total()).astype(BF16)
         stores[2].start()
+        shared_parts[ring.me] = sum_shared.total().astype(BF16)
+        stores[3].start()
         for copy in stores:
             copy.wait()
 
 
 def scan_backward(
-    n, unit, n_ctx, px, ps, kept_parts, d_ssd, gate_t, normed_t, upstream, d_z, mixed_parts, hidden, gain_grads, taps_x, taps_s, skip, head
+    n, unit, n_ctx, px, ps, kept_parts, d_ssd, gate_t, normed_t, upstream, d_z, mixed_parts, hidden, gain_grads, par
 ):
     x, rows_b, rows_c, slope_x, slope_s, lam, step, chain, kept = kept_parts
     tokens, width = px.shape
     heads = width // HEAD
     count = tokens // BLOCK
     own, model = hidden.shape
-    shared_width = ps.shape[1]
     piece = width // n
     assert model == 2 * width and heads // 2 % POINTS == 0
     by_block = lambda i: (count - 1 - i, 0)
@@ -940,7 +990,7 @@
         grid=(count,),
         in_specs=[
             at_block(width),
-            at_block(shared_width),
+            pl.BlockSpec((n_ctx, BLOCK, LANES), lambda i: (0, count - 1 - i, 0)),
             at_block(width),
             at_block(STATE),
             at_block(STATE),
@@ -953,19 +1003,19 @@
             at_block(width),
         ]
         + [any_space] * 6
-        + [whole(a) for a in (gain_grads, taps_x, taps_s, skip, head)],
+        + [whole(a) for a in (gain_grads, par)],
         out_specs=[
             at_block(width),
-            at_block(shared_width),
             pl.BlockSpec(small_shape, lambda i: (0, 0)),
+            any_space,
             any_space,
             any_space,
             any_space,
         ],
         out_shape=[
             low(tokens, width),
-            low(tokens, shared_width),
             jax.ShapeDtypeStruct(small_shape, F32),
+            low(tokens, LANES),
             low(piece, model),
             low(2, width, piece),
             low(own, model),
@@ -990,11 +1040,16 @@
             v_low(2, own, model),
             v_low(2, own, model),
             v_low(own, model),
+            v_low(n_ctx, tokens, LANES),
+            v_low(2, tokens, LANES),
+            v_low(tokens, LANES),
             v_low(own, model),
             dma((4 + 3 * n_ctx,)),
-            dma((3,)),
+            dma((4,)),
             dma((2, 2, 2)),
             dma((2, 2, 2, n - 1)),
+            dma((3,)),
+            dma((3,)),
             dma((3,)),
             dma((3,)),
         ],
@@ -1003,7 +1058,7 @@
         ),
         name="scan_backward",
     )(
-        px, ps, x, rows_b, rows_c, slope_x, slope_s, lam, step, chain, kept, d_ssd, gate_t, normed_t, upstream, d_z, mixed_parts, hidden, gain_grads, taps_x, taps_s, skip, head
+        px, ps, x, rows_b, rows_c, slope_x, slope_s, lam, step, chain, kept, d_ssd, gate_t, normed_t, upstream, d_z, mixed_parts, hidden, gain_grads, par
     )
 
 
@@ -1011,6 +1066,8 @@
     n,
     n_ctx,
     unit,
+    taps,
+    sizes,
     hidden,
     cotangent,
     in_weight_t,
@@ -1019,7 +1076,8 @@
     w_x,
     w_s,
     w_z,
-    small_out,
+    par_out,
+    gain_out,
     proj_x,
     proj_s,
     normed_out,
@@ -1037,7 +1095,12 @@
     out_s,
     out_t,
     v_gain,
+    v_par,
+    conv_lines,
+    gate_line,
+    head_lines,
     load_sem,
+    shared_sem,
     column_sem,
     local_sem,
     keep_sem,
@@ -1074,15 +1137,27 @@
 
     loads = [
         load_columns(inner, raw_x, column_sem.at[0]),
-        [
-            pltpu.make_async_copy(
-                in_weight_t.at[pl.ds(2 * inner, shared)], raw_s.at[pl.ds(0, shared)], load_sem.at[0]
-            )
-        ],
+        [],
         [pltpu.make_async_copy(small, v_small.at[shard], load_sem.at[1])],
         [pltpu.make_async_copy(hidden, v_hidden.at[me], load_sem.at[2])],
         load_columns(0, raw_z, column_sem.at[1]),
     ]
+    raw_s[...] = jnp.zeros_like(raw_s)
+
+    def load_shared(wait):
+        for j in (0, 1):
+            first = me * LANES + j * HEAD
+
+            @pl.when(first < shared)
+            def _():
+                copy = pltpu.make_async_copy(
+                    in_weight_t.at[pl.ds(pl.multiple_of(2 * inner + first, HEAD), HEAD)],
+                    raw_s.at[pl.ds(j * HEAD, HEAD)],
+                    shared_sem.at[j],
+                )
+                copy.wait() if wait else copy.start()
+
+    load_shared(False)
     for copies in loads:
         for copy in copies:
             copy.start()
@@ -1143,12 +1218,12 @@
     v_x[own_rows, :] = raw_x[...].T
     start_stream(phases[0][2])
     start_stream(phases[0][3])
-    loaded(1)
-    raw_s[shared:, :] = jnp.zeros((raw_s.shape[0] - shared, r), BF16)
+    load_shared(True)
     v_s[own_rows, :] = raw_s[...].T
     start_stream(phases[0][1])
     keep_cotangent = pltpu.make_async_copy(cotangent, cotangent_all.at[me], local_sem)
     keep_cotangent.start()
+    keep_shared = pltpu.make_async_copy(out_s, proj_s.at[me], shared_sem.at[2])
     loaded(3)
     loaded(4)
     own_z[...] = raw_z[...].T
@@ -1168,6 +1243,12 @@
                 @pl.when(step < n_ctx)
                 def _():
                     work(step)
+
+                @pl.when(step == n_ctx - 1)
+                def _():
+                    to_row(2, out_s, proj_s).start()
+                    to_core(2, out_s, proj_s).start()
+                    keep_shared.start()
 
             return carry
 
@@ -1196,9 +1277,9 @@
             (
                 (v_x, w_x),
                 (v_s, w_s),
-                (v_small, small_out),
+                (v_par, par_out),
+                (v_gain, gain_out),
                 (out_x, proj_x),
-                (out_s, proj_s),
                 (v_normed, normed_out),
                 (out_t, normed_t),
             )
@@ -1219,43 +1300,84 @@
     def after_second():
         to_row(1, cotangent, cotangent_all).wait_recv()
         pass_on(1, cotangent_all).start()
-        for copy in stores[3:]:
+        to_row(2, out_s, proj_s).wait_recv()
+        pass_on(2, proj_s).start()
+        for copy in stores[4:]:
             copy.start()
 
     run_phase(0, None, after_first)
+    gain_size, conv_size, gate_size, held = sizes
+    head_lines[...] = jnp.zeros_like(head_lines)
     for f in range(n):
         v_gain[:, f * r : (f + 1) * r] = v_small[f, 0:1, 0:r].astype(F32)
-    for copy in stores[0:3]:
+        conv_lines[0 : taps + 1, f * conv_size : (f + 1) * conv_size] = v_small[
+            f, 1 : taps + 2, 0:conv_size
+        ].astype(F32)
+        gate_line[:, f * gate_size : (f + 1) * gate_size] = v_small[
+            f, taps + 2 : taps + 3, 0:gate_size
+        ].astype(F32)
+        for k in range(3):
+            head_lines[k : k + 1, f * held : (f + 1) * held] = v_small[
+                f, taps + 3 : taps + 4, k * held : (k + 1) * held
+            ].astype(F32)
+
+    def own_part(line, a):
+        at = (a * n_ctx + me) * part
+        span = max(part, LANES)
+        found = line[:, pl.ds(pl.multiple_of(at // LANES * LANES, LANES), span)]
+        if part < LANES:
+            found = pltpu.roll(found, lax.rem(LANES - at % LANES, LANES), 1)
+        return found[:, 0:part]
+
+    v_par[...] = jnp.zeros_like(v_par)
+    for a in range(width // part):
+        v_par[0 : taps + 1, a * part : (a + 1) * part] = own_part(conv_lines, a)[0 : taps + 1]
+        v_par[taps + 1 : taps + 2, a * part : (a + 1) * part] = own_part(gate_line, a)
+    v_par[0 : taps + 1, width:] = conv_lines[0 : taps + 1, inner:]
+    lines = mm(head_lines[...].astype(BF16), chosen_heads(me, width // HEAD, unit, n_ctx))
+    heads_row = taps + 3
+    v_par[heads_row : heads_row + 1, 0:LANES] = lines[0:1]
+    v_par[heads_row : heads_row + 1, LANES : 2 * LANES] = jnp.exp(lines[1:2])
+    wide = (iota2((LANES, width), 1) // HEAD == iota2((LANES, width), 0)).astype(BF16)
+    v_par[taps + 2 : taps + 3, 0:width] = mm(lines.astype(BF16), wide)[2:3]
+    for copy in stores[0:4]:
         copy.start()
     run_phase(1, project_first, after_second)
     to_row(1, cotangent, cotangent_all).wait_send()
     to_core(1, cotangent, cotangent_all).wait()
     pass_on(1, cotangent_all).wait()
     keep_cotangent.wait()
+    to_row(2, out_s, proj_s).wait_send()
+    to_core(2, out_s, proj_s).wait()
+    pass_on(2, proj_s).wait()
+    keep_shared.wait()
     for copy in stores:
         copy.wait()
 
 
-def gather_all(n, n_ctx, unit, width, hidden, cotangent, in_weight_t, small, shared_width):
+def gather_all(n, n_ctx, unit, taps, sizes, width, hidden, cotangent, in_weight_t, small):
     own, model = hidden.shape
     tokens = own * n_ctx
     rows = in_weight_t.shape[1]
     any_space = pl.BlockSpec(memory_space=pl.ANY)
+    par_shape = (taps + 4, width + 2 * STATE)
+    inner = width * n_ctx
     low = lambda *shape: jax.ShapeDtypeStruct(shape, BF16)
     v_low = lambda *shape: pltpu.VMEM(shape, BF16)
     dma = pltpu.SemaphoreType.DMA
     return pl.pallas_call(
-        functools.partial(gather_kernel, n, n_ctx, unit),
+        functools.partial(gather_kernel, n, n_ctx, unit, taps, sizes),
         in_specs=[any_space] * 4,
-        out_specs=[any_space] * 9,
+        out_specs=[any_space] * 10,
         out_shape=[
             low(n_ctx, own, model),
             low(model, width),
-            low(model, shared_width),
+            low(model, LANES),
             low(model, width),
-            low(n, small.shape[0], small.shape[1]),
+            jax.ShapeDtypeStruct(par_shape, F32),
+            jax.ShapeDtypeStruct((1, model), F32),
             low(tokens, width),
-            low(tokens, shared_width),
+            low(n_ctx, tokens, LANES),
             low(tokens, model),
             low(n_ctx, model, own),
         ],
@@ -1263,16 +1385,21 @@
             v_low(n_ctx, own, model),
             v_low(tokens, model),
             v_low(model, width),
-            v_low(model, shared_width),
+            v_low(model, LANES),
             v_low(rows, width),
             v_low(n, small.shape[0], small.shape[1]),
             v_low(width, rows),
-            v_low(shared_width, rows),
+            v_low(LANES, rows),
             v_low(width, rows),
             v_low(tokens, width),
-            v_low(tokens, shared_width),
+            v_low(tokens, LANES),
             v_low(n_ctx, model, own),
             pltpu.VMEM((1, model), F32),
+            pltpu.VMEM(par_shape, F32),
+            pltpu.VMEM((8, inner + 2 * STATE), F32),
+            pltpu.VMEM((1, inner), F32),
+            pltpu.VMEM((8, LANES), F32),
+            dma((3,)),
             dma((3,)),
             dma((2, width // (unit * HEAD))),
             dma,
@@ -1280,8 +1407,8 @@
             dma((7,)),
             dma((6, 2)),
             dma((6, 2, n - 1)),
-            dma((2, 3)),
-            dma((2, 3)),
+            dma((3, 3)),
+            dma((3, 3)),
         ],
         compiler_params=pltpu.CompilerParams(
             collective_id=0, has_side_effects=True, vmem_limit_bytes=56 * 1024 * 1024
@@ -1663,7 +1790,7 @@
     )
 
 
-def assemble_kernel(part, z_ref, x_ref, s_ref, out_ref):
+def assemble_kernel(part, z_ref, x_ref, s_ref, o_ref, out_ref, rows_ref):
     place = pl.program_id(0)
     n_ctx, size, half = x_ref.shape[0], x_ref.shape[1], z_ref.shape[3]
 
@@ -1693,15 +1820,20 @@
 
     @pl.when(place == 2 * n_ctx)
     def _():
-        total = s_ref[0].astype(F32)
-        for c in range(1, n_ctx):
-            total += s_ref[c].astype(F32)
-        out_ref[0 : total.shape[0], :] = total
-
-
-def assemble(part, g_z, g_x, g_s, columns):
+        for c in range(s_ref.shape[0]):
+            out_ref[c * LANES : (c + 1) * LANES, :] = s_ref[c].astype(F32)
+
+    @pl.when(place < 2 * n_ctx)
+    def _():
+        rows_ref[...] = o_ref[...].astype(F32)
+
+
+def assemble(part, g_z, g_x, g_s, g_o, columns):
     n_ctx, width, rows = g_x.shape
     block = (n_ctx, width // n_ctx, rows)
+    g_o = g_o.reshape(-1, g_o.shape[2])
+    tile = max(g_o.shape[0] // (2 * n_ctx), 16)
+    at_tile = lambda i: (jnp.minimum(i, g_o.shape[0] // tile - 1), 0)
     return pl.pallas_call(
         functools.partial(assemble_kernel, part),
         grid=(2 * n_ctx + 1,),
@@ -1712,12 +1844,19 @@
             ),
             pl.BlockSpec(block, lambda i: (0, jnp.clip(i - n_ctx, 0, n_ctx - 1), 0)),
             pl.BlockSpec(g_s.shape, lambda i: (0, 0, 0)),
+            pl.BlockSpec((tile, g_o.shape[1]), at_tile),
         ],
-        out_specs=pl.BlockSpec((width, rows), lambda i: (i, 0)),
-        out_shape=jax.ShapeDtypeStruct((columns, rows), F32),
+        out_specs=[
+            pl.BlockSpec((width, rows), lambda i: (i, 0)),
+            pl.BlockSpec((tile, g_o.shape[1]), at_tile),
+        ],
+        out_shape=[
+            jax.ShapeDtypeStruct((columns, rows), F32),
+            jax.ShapeDtypeStruct(g_o.shape, F32),
+        ],
         compiler_params=pltpu.CompilerParams(vmem_limit_bytes=58 * 1024 * 1024),
         name="assemble",
-    )(g_z, g_x, g_s)
+    )(g_z, g_x, g_s, g_o)
 
 
 def on_device(
@@ -1746,45 +1885,29 @@
     direct = held % n_ctx == 0
     unit = held // n_ctx if direct else 1
     part = unit * HEAD
-    shared_width = -(-(both + heads_all) // LANES) * LANES
+    assert both + heads_all <= n_ctx * LANES and heads_all == HEAD
 
     per_head = jnp.concatenate([dt_bias, a_log, d_skip])
     lines = [norm_gain[None], conv_weight, conv_bias[None], gate_gain[None], per_head[None]]
     longest = -(-max(a.shape[1] for a in lines) // LANES) * LANES
     small = jnp.concatenate([jnp.pad(a, ((0, 0), (0, longest - a.shape[1]))) for a in lines])
     small = jnp.pad(small, ((0, SMALL_ROWS - small.shape[0]), (0, 0)))
-    upstream, w_x, w_s, w_z, small_all, proj_x, proj_s, normed, normed_t = gather_all(
-        n_fsdp, n_ctx, unit, width, hidden[0], cotangent[0], in_weight.T, small, shared_width
-    )
-
-    def line(first, count, size):
-        rows = small_all[:, first : first + count, :size]
-        return jnp.moveaxis(rows, 0, 1).reshape(count, -1).astype(F32)
-
-    def own(lines, size):
-        by_part = lines.reshape(lines.shape[0], -1, n_ctx, size)
-        return lax.dynamic_index_in_dim(by_part, me, 2, False).reshape(lines.shape[0], -1)
-
-    gain_norm = line(0, 1, norm_gain.shape[0])
-    conv_lines = line(1, taps + 1, conv_bias.shape[0])
-    taps_x, taps_s = own(conv_lines[:, :inner], part), conv_lines[:, inner:]
-    gain_gate = own(line(taps + 2, 1, gate_gain.shape[0]), part)
-    each = small_all[:, taps + 3, : per_head.shape[0]].reshape(n_fsdp, 3, -1)
-    each = own(jnp.moveaxis(each, 0, 1).reshape(3, -1).astype(F32), unit)
-    head = jnp.pad(jnp.stack([each[0], jnp.exp(each[1])]), ((0, 0), (0, LANES - heads)))
-    skip = jnp.repeat(each[2], HEAD)[None]
-
+    sizes = (norm_gain.shape[0], conv_bias.shape[0], gate_gain.shape[0], held)
+    upstream, w_x, w_s, w_z, par, gain_norm, proj_x, proj_s, normed, normed_t = gather_all(
+        n_fsdp, n_ctx, unit, taps, sizes, width, hidden[0], cotangent[0], in_weight.T, small
+    )
     *kept_parts, gain_grads, gate_t, mixed_parts, d_z, d_ssd = scan_forward(
-        n_fsdp, direct, unit, n_ctx, seq_lens, proj_x, proj_s, normed, out_weight, w_z, upstream, taps_x, taps_s, gain_gate, skip, head
-    )
-    d_x, d_s, small_grads, shard_o, shard_z, layer_out = scan_backward(
-        n_fsdp, unit, n_ctx, proj_x, proj_s, kept_parts, d_ssd, gate_t, normed_t, upstream, d_z, mixed_parts, hidden[0], gain_grads, taps_x, taps_s, skip, head
+        n_fsdp, direct, unit, n_ctx, seq_lens, proj_x, proj_s, normed, out_weight, w_z, upstream, par
+    )
+    d_x, small_grads, d_s, shard_o, shard_z, layer_out = scan_backward(
+        n_fsdp, unit, n_ctx, proj_x, proj_s, kept_parts, d_ssd, gate_t, normed_t, upstream, d_z, mixed_parts, hidden[0], gain_grads, par
     )
     g_z, g_x, g_s, g_o, hidden_grad, sums, norm_sums = reduce_all(
         n_fsdp, n_ctx, direct, normed_t, d_z, d_x, d_s, w_z, w_x, w_s, shard_o, shard_z, small_grads, hidden[0], cotangent[0], gain_norm
     )
-    grad_in_weight = assemble(part, g_z, g_x, g_s, 2 * inner + both + heads_all).T
-    grad_out_weight = g_o.reshape(-1, model).astype(F32)
+    grad_in_weight, grad_out_weight = assemble(
+        part, g_z, g_x, g_s, g_o, 2 * inner + both + heads_all
+    )
 
     def shard_of(lines):
         size = lines.shape[1] // n_fsdp
@@ -1812,7 +1935,7 @@
         layer_out[None],
         hidden_grad[None],
         shard_of(norm_sums)[0],
-        grad_in_weight,
+        grad_in_weight.T,
         conv_sums[:taps],
         conv_sums[taps],
         head_grads[0],

time: 401 us -> 369 us (0.920); the launches traced: 395 us -> 367 us
  Pallas kernels: 366 us -> 353 us
  other arithmetic: 10.2 us -> 1.62 us
  local copies, waits for them, and re-layouts: 16.4 us -> 11.6 us
    pallas_call x1, Pallas kernels: 102 us -> 92.3 us  [gather_all(): pl.pallas_call(functools.partial(gather_kernel, n, n_ctx, unit, taps, siz...]
    pallas_call x1, Pallas kernels: 83.4 us -> 75.1 us  [reduce_all(): pl.pallas_call(functools.partial(reduce_kernel, n, n_ctx, direct), in_spe...]
    convert_element_type x5 -> x0, other arithmetic: 7.23 us -> none  [the longest x1 4.13 us: on_device(): grad_out_weight = g_o.reshape(-1, model).astype(F32)]
where the time goes in v2:
time: 369 us; the launch traced here: 367 us
  Pallas kernels  353 us (96%)
  local copies, waits for them, and re-layouts  11.6 us (3%)
    pallas_call x1, Pallas kernels, scan_backward(): pl.pallas_call(functools.partial(backward_kernel, heads, unit, n_ctx, n),...  104 us
    pallas_call x1, Pallas kernels, gather_all(): pl.pallas_call(functools.partial(gather_kernel, n, n_ctx, unit, taps, siz...  92.3 us
    pallas_call x1, Pallas kernels, reduce_all(): pl.pallas_call(functools.partial(reduce_kernel, n, n_ctx, direct), in_spe...  75.1 us
    pallas_call x1, Pallas kernels, scan_forward(): pl.pallas_call(functools.partial(forward_kernel, heads, unit, n_ctx, n, d...  72 us
    pallas_call x1, Pallas kernels, assemble(): pl.pallas_call(functools.partial(assemble_kernel, part), grid=(2 * n_ctx...  9.6 us

profile of v2, /device:TPU:17, one launch (start us, length us, event | category | flops | bytes accessed | tf_op | source)
XLA Modules:
  0.0 367.3 jit_solution(17269610436278360615)
XLA Ops:
  0.6 0.7 pad.25
  1.3 0.7 broadcast_in_dim.19
  2.0 0.7 broadcast_in_dim.20
  2.7 0.7 broadcast_in_dim.18
  3.4 0.8 maximum_bitcast_fusion
  4.2 0.6 pad.29.small
  4.8 92.3 %gather_all.1 = (bf16[4,256,2048]{2,1,0:T(8,128)(2,1)}, bf16[2048,1024]{1,0:T(8,128)(2,1)}, bf16[2048,128]{1,0:T(8,128)(2,1)}, bf16[2048,1024]{1,0:T(8,128)(2,1)...) custom-call(bf16[256,2048]{1,0:T(8,128)(2,1)} %bitcast.33, ...), custom_call_target="tpu_custom_call" | custom-call | tf_op jit(solution)/shard_map/gather_all/pallas_call | solution.py:1368
  97.8 72.0 %scan_forward.1 = (bf16[1024,1024]{1,0:T(8,128)(2,1)}, bf16[1024,128]{1,0:T(8,128)(2,1)}, bf16[1024,128]{1,0:T(8,128)(2,1)}, bf16[1024,1024]{1,0:T(8,128)(2,1)},...) custom-call(s32[1]{0:T(128)S(6)} %copy.43.length_ref, ...), custom_call_target="tpu_custom_call" | custom-call | tf_op jit(solution)/shard_map/scan_forward/pallas_call | solution.py:521
  169.8 103.5 %scan_backward.1 = (bf16[1024,1024]{1,0:T(8,128)(2,1)}, f32[8,1280]{1,0:T(8,128)}, bf16[1024,128]{1,0:T(8,128)(2,1)}, bf16[128,2048]{1,0:T(8,128)(2,1)}, bf16[2,...) custom-call(bf16[1024,1024]{1,0:T(8,128)(2,1)} %get-tuple-element.50.px_ref, ...), custom_call_target="tpu_custom_call" | custom-call | tf_op jit(solution)/shard_map/scan_backward/pallas_call | solution.py:988
  273.4 75.1 %reduce_all.1 = (bf16[4,2,1024,128]{3,2,1,0:T(8,128)(2,1)}, bf16[4,1024,256]{2,1,0:T(8,128)(2,1)}, bf16[4,128,256]{2,1,0:T(8,128)(2,1)}, bf16[4,128,2048]{2,1,0:...) custom-call(bf16[4,2048,256]{2,1,0:T(8,128)(2,1)} %get-tuple-element.67.normed_t, ...), custom_call_target="tpu_custom_call" | custom-call | tf_op jit(solution)/shard_map/reduce_all/pallas_call | solution.py:1732
  348.5 0.9 slice.30
  349.5 0.8 slice_reduce_fusion
  350.3 0.1 fusion
  350.4 0.6 slice.40
  351.0 0.6 slice_reduce_fusion.1
  351.6 0.0 copy-start.2
  351.6 0.0 copy-start
  351.6 9.6 %assemble.1 = (f32[8512,256]{1,0:T(8,128)}, f32[512,2048]{1,0:T(8,128)}) custom-call(bf16[4,2,1024,128]{3,2,1,0:T(8,128)(2,1)} %get-tuple-element.82.z_ref, bf16[4,1024,256]{2,1,0:T(8,128)(2,1)} %get-tuple-element.83.x_ref, bf16[4,128,256]{2,1,0:T(8,128)(2,1)} %get-tuple-element.84.s_ref, bf16[512,2048]{1,0:T(8,128)(2,1)} %bitcast.39), custom_call_target="tpu_custom_call" | custom-call | tf_op jit(solution)/shard_map/assemble/pallas_call | solution.py:1837
  361.2 0.0 copy-start.1
  361.2 0.9 slice.34
  362.1 0.1 copy.33
  362.2 0.3 copy.34
  362.5 0.1 reshape.51
  362.6 0.1 constant_dynamic-slice_fusion.1
  362.6 0.5 slice_bitcast_fusion
  363.2 0.9 slice.39
  364.1 0.6 constant_dynamic-slice_fusion
  364.7 0.0 copy-done.2
  364.7 0.6 constant_dynamic-slice_fusion.2
  365.3 0.0 copy-done
  365.3 1.0 copy.44
  366.3 0.0 copy-done.1
  366.3 1.0 copy.45
  (12 shorter events, 0.2 us)
Async XLA Ops:
  351.6 13.1 %copy-start.2 = (f32[4,8,256]{2,1,0:T(8,128)S(1)}, f32[4,8,256]{2,1,0:T(8,128)}, u32[]{:S(2)}) copy-start(f32[4,8,256]{2,1,0:T(8,128)} %get-tuple-element.81) | copy-start | bytes 98308
  351.6 13.7 %copy-start = (bf16[256,2048]{1,0:T(8,128)(2,1)S(1)}, bf16[256,2048]{1,0:T(8,128)(2,1)}, u32[]{:S(2)}) copy-start(bf16[256,2048]{1,0:T(8,128)(2,1)} %get-tuple-element.71) | copy-start | bytes 3145732
  361.2 5.1 %copy-start.1 = (bf16[256,2048]{1,0:T(8,128)(2,1)S(1)}, bf16[256,2048]{1,0:T(8,128)(2,1)}, u32[]{:S(2)}) copy-start(bf16[256,2048]{1,0:T(8,128)(2,1)} %get-tuple-element.80) | copy-start | bytes 3145732

commit v3 on v2

--- a/solution.py
+++ b/solution.py
@@ -257,6 +257,7 @@
     all_y,
     all_z,
     all_dyn,
+    all_g,
     v_yt,
     v_mixed,
     v_dz,
@@ -428,7 +429,9 @@
             all_dyn[chunk] = d_yn
             gated = all_y[chunk] * jax.nn.silu(all_z[chunk].astype(F32))
             square = jnp.sum(gated * gated, axis=1, keepdims=True)
-            along = jnp.sum(gate_gain_ref[...] * d_yn * gated, axis=1, keepdims=True)
+            weighted = gate_gain_ref[...] * gated
+            all_g[chunk] = weighted.astype(BF16)
+            along = jnp.sum(weighted * d_yn, axis=1, keepdims=True)
             pair = jnp.where(lane == 0, square, 0.0) + jnp.where(lane == 1, along, 0.0)
             stat_all[me, chunk] = pair.T[0:8]
             return carry
@@ -442,11 +445,32 @@
         for copy in copies:
             copy.start()
         gain_ref[...] = jnp.zeros_like(gain_ref)
+
+        def store_mixed(chunk):
+            slot = chunk % 2
+            return pltpu.make_async_copy(
+                v_mixed.at[slot], mixed_parts.at[chunk], store_sem.at[slot, 3]
+            )
+
+        def mixed_of(chunk, carry):
+            @pl.when(chunk >= 2)
+            def _():
+                store_mixed(chunk - 2).wait()
+
+            v_mixed[chunk % 2] = mm(all_g[chunk], v_o[...]).astype(BF16)
+            store_mixed(chunk).start()
+            return carry
+
+        lax.fori_loop(0, blocks, mixed_of, 0)
         for copy in copies:
             copy.wait()
         total = jnp.sum(stat_all[...], axis=0)
         for i in range(n_ctx):
             columns[i] = total[i].T
+        own_total = sum(stat_all[c, me] for c in range(n_ctx))
+        own_valid = iota2((1, BLOCK), 1) + me * BLOCK < length_ref[0]
+        scale_row = lax.rsqrt(own_total[0:1] / channels + EPS)
+        gain_ref[1:2, 0:BLOCK] = jnp.where(own_valid, scale_row, 0.0)
 
         def stores(chunk):
             slot = chunk % 2
@@ -456,7 +480,6 @@
                 for i, (source, target) in enumerate(
                     (
                         (v_yt, gate_t.at[chunk]),
-                        (v_mixed, mixed_parts.at[chunk]),
                         (v_dz, d_z.at[rows]),
                         (v_dssd, d_ssd.at[rows]),
                     )
@@ -488,9 +511,7 @@
                 d_gated = scale * (gain * d_yn) - gated * slant
                 v_dz[slot, :, lanes] = (d_gated * mixed * gate_slope).astype(BF16)
                 v_dssd[slot, :, lanes] = (d_gated * gate).astype(BF16)
-            normed_gate = all_z[chunk]
-            v_yt[slot] = normed_gate.T
-            v_mixed[slot] = mm(normed_gate, v_o[...]).astype(BF16)
+            v_yt[slot] = all_z[chunk].T
             for copy in stores(chunk):
                 copy.start()
             return carry
@@ -499,6 +520,7 @@
         for chunk in (n_ctx - 2, n_ctx - 1):
             for copy in stores(chunk):
                 copy.wait()
+            store_mixed(chunk).wait()
 
 
 def scan_forward(
@@ -573,6 +595,7 @@
             v_full(count, BLOCK, width),
             v_low(count, BLOCK, width),
             v_full(count, BLOCK, width),
+            v_low(count, BLOCK, width),
             v_low(2, width, BLOCK),
             v_low(2, BLOCK, model),
             v_low(2, BLOCK, width),
@@ -957,7 +980,9 @@
         ]
         stores[0].start()
         stores[1].start()
-        v_hidden[...] = (v_hidden[...].astype(F32) + sum_mixed.total()).astype(BF16)
+        scale = gain_grads_ref[:, 0:BLOCK].T[:, 1:2]
+        total = v_hidden[...].astype(F32) + scale * sum_mixed.total()
+        v_hidden[...] = total.astype(BF16)
         stores[2].start()
         shared_parts[ring.me] = sum_shared.total().astype(BF16)
         stores[3].start()

time: 369 us -> 374 us (1.014)
  Pallas kernels: 353 us -> 359 us
    pallas_call x1, Pallas kernels: 104 us -> 115 us  [scan_backward(): pl.pallas_call(functools.partial(backward_kernel, heads, unit, n_ctx, n),...]
    pallas_call x1, Pallas kernels: 72 us -> 67.6 us  [scan_forward(): pl.pallas_call(functools.partial(forward_kernel, heads, unit, n_ctx, n, d...]
where the time goes in v3:
time: 374 us
  Pallas kernels  359 us (96%)
  local copies, waits for them, and re-layouts  11.6 us (3%)
    pallas_call x1, Pallas kernels, scan_backward(): pl.pallas_call(functools.partial(backward_kernel, heads, unit, n_ctx, n),...  115 us
    pallas_call x1, Pallas kernels, gather_all(): pl.pallas_call(functools.partial(gather_kernel, n, n_ctx, unit, taps, siz...  92.3 us
    pallas_call x1, Pallas kernels, reduce_all(): pl.pallas_call(functools.partial(reduce_kernel, n, n_ctx, direct), in_spe...  75.1 us
    pallas_call x1, Pallas kernels, scan_forward(): pl.pallas_call(functools.partial(forward_kernel, heads, unit, n_ctx, n, d...  67.6 us
    pallas_call x1, Pallas kernels, assemble(): pl.pallas_call(functools.partial(assemble_kernel, part), grid=(2 * n_ctx...  9.6 us

profile of v3, /device:TPU:17, one launch (start us, length us, event | category | flops | bytes accessed | tf_op | source)
XLA Modules:
  0.0 374.0 jit_solution(4492015696751818974)
XLA Ops:
  0.6 0.7 pad.25
  1.3 0.7 broadcast_in_dim.19
  2.0 0.7 broadcast_in_dim.20
  2.7 0.7 broadcast_in_dim.18
  3.4 0.8 maximum_bitcast_fusion
  4.2 0.6 pad.29.small
  4.8 92.3 %gather_all.1 = (bf16[4,256,2048]{2,1,0:T(8,128)(2,1)}, bf16[2048,1024]{1,0:T(8,128)(2,1)}, bf16[2048,128]{1,0:T(8,128)(2,1)}, bf16[2048,1024]{1,0:T(8,128)(2,1)...) custom-call(bf16[256,2048]{1,0:T(8,128)(2,1)} %bitcast.33, ...), custom_call_target="tpu_custom_call" | custom-call | tf_op jit(solution)/shard_map/gather_all/pallas_call | solution.py:1393
  97.8 67.6 %scan_forward.1 = (bf16[1024,1024]{1,0:T(8,128)(2,1)}, bf16[1024,128]{1,0:T(8,128)(2,1)}, bf16[1024,128]{1,0:T(8,128)(2,1)}, bf16[1024,1024]{1,0:T(8,128)(2,1)},...) custom-call(s32[1]{0:T(128)S(6)} %copy.43.length_ref, ...), custom_call_target="tpu_custom_call" | custom-call | tf_op jit(solution)/shard_map/scan_forward/pallas_call | solution.py:543
  165.4 114.5 %scan_backward.1 = (bf16[1024,1024]{1,0:T(8,128)(2,1)}, f32[8,1280]{1,0:T(8,128)}, bf16[1024,128]{1,0:T(8,128)(2,1)}, bf16[128,2048]{1,0:T(8,128)(2,1)}, bf16[2,...) custom-call(bf16[1024,1024]{1,0:T(8,128)(2,1)} %get-tuple-element.50.px_ref, ...), custom_call_target="tpu_custom_call" | custom-call | tf_op jit(solution)/shard_map/scan_backward/pallas_call | solution.py:1013
  279.9 75.1 %reduce_all.1 = (bf16[4,2,1024,128]{3,2,1,0:T(8,128)(2,1)}, bf16[4,1024,256]{2,1,0:T(8,128)(2,1)}, bf16[4,128,256]{2,1,0:T(8,128)(2,1)}, bf16[4,128,2048]{2,1,0:...) custom-call(bf16[4,2048,256]{2,1,0:T(8,128)(2,1)} %get-tuple-element.67.normed_t, ...), custom_call_target="tpu_custom_call" | custom-call | tf_op jit(solution)/shard_map/reduce_all/pallas_call | solution.py:1757
  355.1 0.9 slice.30
  356.1 0.8 slice_reduce_fusion
  356.9 0.1 fusion
  356.9 0.6 slice.40
  357.6 0.6 slice_reduce_fusion.1
  358.2 0.0 copy-start.2
  358.2 0.0 copy-start
  358.2 9.6 %assemble.1 = (f32[8512,256]{1,0:T(8,128)}, f32[512,2048]{1,0:T(8,128)}) custom-call(bf16[4,2,1024,128]{3,2,1,0:T(8,128)(2,1)} %get-tuple-element.82.z_ref, bf16[4,1024,256]{2,1,0:T(8,128)(2,1)} %get-tuple-element.83.x_ref, bf16[4,128,256]{2,1,0:T(8,128)(2,1)} %get-tuple-element.84.s_ref, bf16[512,2048]{1,0:T(8,128)(2,1)} %bitcast.39), custom_call_target="tpu_custom_call" | custom-call | tf_op jit(solution)/shard_map/assemble/pallas_call | solution.py:1862
  367.8 0.0 copy-start.1
  367.8 0.9 slice.34
  368.7 0.1 copy.33
  368.8 0.3 copy.34
  369.0 0.1 reshape.51
  369.1 0.1 constant_dynamic-slice_fusion.1
  369.2 0.5 slice_bitcast_fusion
  369.7 0.9 slice.39
  370.7 0.6 constant_dynamic-slice_fusion
  371.3 0.0 copy-done.2
  371.3 0.6 constant_dynamic-slice_fusion.2
  371.9 0.0 copy-done
  371.9 1.0 copy.44
  372.8 0.0 copy-done.1
  372.8 1.0 copy.45
  (12 shorter events, 0.2 us)
Async XLA Ops:
  358.2 13.1 %copy-start.2 = (f32[4,8,256]{2,1,0:T(8,128)S(1)}, f32[4,8,256]{2,1,0:T(8,128)}, u32[]{:S(2)}) copy-start(f32[4,8,256]{2,1,0:T(8,128)} %get-tuple-element.81) | copy-start | bytes 98308
  358.2 13.7 %copy-start = (bf16[256,2048]{1,0:T(8,128)(2,1)S(1)}, bf16[256,2048]{1,0:T(8,128)(2,1)}, u32[]{:S(2)}) copy-start(bf16[256,2048]{1,0:T(8,128)(2,1)} %get-tuple-element.71) | copy-start | bytes 3145732
  367.8 5.1 %copy-start.1 = (bf16[256,2048]{1,0:T(8,128)(2,1)S(1)}, bf16[256,2048]{1,0:T(8,128)(2,1)}, u32[]{:S(2)}) copy-start(bf16[256,2048]{1,0:T(8,128)(2,1)} %get-tuple-element.80) | copy-start | bytes 3145732

commit v4 on v2

--- a/solution.py
+++ b/solution.py
@@ -11,7 +11,7 @@
 STATE = 128
 BLOCK = 256
 LANES = 128
-POINTS = 4
+POINTS = 8
 EPS = 1e-05
 F32 = jnp.float32
 BF16 = jnp.bfloat16

time: 369 us -> 367 us (level)
  no operation moved by 1% of the time
where the time goes in v4:
time: 367 us; the launch traced here: 366 us
  Pallas kernels  352 us (96%)
  local copies, waits for them, and re-layouts  11.6 us (3%)
    pallas_call x1, Pallas kernels, scan_backward(): pl.pallas_call(functools.partial(backward_kernel, heads, unit, n_ctx, n),...  103 us
    pallas_call x1, Pallas kernels, gather_all(): pl.pallas_call(functools.partial(gather_kernel, n, n_ctx, unit, taps, siz...  92.3 us
    pallas_call x1, Pallas kernels, reduce_all(): pl.pallas_call(functools.partial(reduce_kernel, n, n_ctx, direct), in_spe...  75.2 us
    pallas_call x1, Pallas kernels, scan_forward(): pl.pallas_call(functools.partial(forward_kernel, heads, unit, n_ctx, n, d...  72 us
    pallas_call x1, Pallas kernels, assemble(): pl.pallas_call(functools.partial(assemble_kernel, part), grid=(2 * n_ctx...  9.6 us

profile of v4, /device:TPU:17, one launch (start us, length us, event | category | flops | bytes accessed | tf_op | source)
XLA Modules:
  0.0 366.2 jit_solution(6711113471802956293)
XLA Ops:
  0.6 0.7 pad.25
  1.3 0.7 broadcast_in_dim.19
  2.0 0.7 broadcast_in_dim.20
  2.7 0.7 broadcast_in_dim.18
  3.4 0.8 maximum_bitcast_fusion
  4.2 0.6 pad.29.small
  4.8 92.3 %gather_all.1 = (bf16[4,256,2048]{2,1,0:T(8,128)(2,1)}, bf16[2048,1024]{1,0:T(8,128)(2,1)}, bf16[2048,128]{1,0:T(8,128)(2,1)}, bf16[2048,1024]{1,0:T(8,128)(2,1)...) custom-call(bf16[256,2048]{1,0:T(8,128)(2,1)} %bitcast.33, ...), custom_call_target="tpu_custom_call" | custom-call | tf_op jit(solution)/shard_map/gather_all/pallas_call | solution.py:1368
  97.8 72.0 %scan_forward.1 = (bf16[1024,1024]{1,0:T(8,128)(2,1)}, bf16[1024,128]{1,0:T(8,128)(2,1)}, bf16[1024,128]{1,0:T(8,128)(2,1)}, bf16[1024,1024]{1,0:T(8,128)(2,1)},...) custom-call(s32[1]{0:T(128)S(6)} %copy.43.length_ref, ...), custom_call_target="tpu_custom_call" | custom-call | tf_op jit(solution)/shard_map/scan_forward/pallas_call | solution.py:521
  169.8 102.5 %scan_backward.1 = (bf16[1024,1024]{1,0:T(8,128)(2,1)}, f32[8,1280]{1,0:T(8,128)}, bf16[1024,128]{1,0:T(8,128)(2,1)}, bf16[128,2048]{1,0:T(8,128)(2,1)}, bf16[2,...) custom-call(bf16[1024,1024]{1,0:T(8,128)(2,1)} %get-tuple-element.50.px_ref, ...), custom_call_target="tpu_custom_call" | custom-call | tf_op jit(solution)/shard_map/scan_backward/pallas_call | solution.py:988
  272.3 75.2 %reduce_all.1 = (bf16[4,2,1024,128]{3,2,1,0:T(8,128)(2,1)}, bf16[4,1024,256]{2,1,0:T(8,128)(2,1)}, bf16[4,128,256]{2,1,0:T(8,128)(2,1)}, bf16[4,128,2048]{2,1,0:...) custom-call(bf16[4,2048,256]{2,1,0:T(8,128)(2,1)} %get-tuple-element.67.normed_t, ...), custom_call_target="tpu_custom_call" | custom-call | tf_op jit(solution)/shard_map/reduce_all/pallas_call | solution.py:1732
  347.5 0.9 slice.30
  348.5 0.8 slice_reduce_fusion
  349.3 0.1 fusion
  349.4 0.6 slice.40
  350.0 0.6 slice_reduce_fusion.1
  350.6 0.0 copy-start.2
  350.6 0.0 copy-start
  350.6 9.6 %assemble.1 = (f32[8512,256]{1,0:T(8,128)}, f32[512,2048]{1,0:T(8,128)}) custom-call(bf16[4,2,1024,128]{3,2,1,0:T(8,128)(2,1)} %get-tuple-element.82.z_ref, bf16[4,1024,256]{2,1,0:T(8,128)(2,1)} %get-tuple-element.83.x_ref, bf16[4,128,256]{2,1,0:T(8,128)(2,1)} %get-tuple-element.84.s_ref, bf16[512,2048]{1,0:T(8,128)(2,1)} %bitcast.39), custom_call_target="tpu_custom_call" | custom-call | tf_op jit(solution)/shard_map/assemble/pallas_call | solution.py:1837
  360.2 0.0 copy-start.1
  360.2 0.9 slice.34
  361.1 0.1 copy.33
  361.2 0.3 copy.34
  361.5 0.1 reshape.51
  361.6 0.1 constant_dynamic-slice_fusion.1
  361.6 0.5 slice_bitcast_fusion
  362.2 0.9 slice.39
  363.1 0.6 constant_dynamic-slice_fusion
  363.7 0.0 copy-done.2
  363.7 0.6 constant_dynamic-slice_fusion.2
  364.3 0.0 copy-done
  364.3 1.0 copy.44
  365.3 0.0 copy-done.1
  365.3 1.0 copy.45
  (12 shorter events, 0.2 us)
Async XLA Ops:
  350.6 13.1 %copy-start.2 = (f32[4,8,256]{2,1,0:T(8,128)S(1)}, f32[4,8,256]{2,1,0:T(8,128)}, u32[]{:S(2)}) copy-start(f32[4,8,256]{2,1,0:T(8,128)} %get-tuple-element.81) | copy-start | bytes 98308
  350.6 13.7 %copy-start = (bf16[256,2048]{1,0:T(8,128)(2,1)S(1)}, bf16[256,2048]{1,0:T(8,128)(2,1)}, u32[]{:S(2)}) copy-start(bf16[256,2048]{1,0:T(8,128)(2,1)} %get-tuple-element.71) | copy-start | bytes 3145732
  360.2 5.1 %copy-start.1 = (bf16[256,2048]{1,0:T(8,128)(2,1)S(1)}, bf16[256,2048]{1,0:T(8,128)(2,1)}, u32[]{:S(2)}) copy-start(bf16[256,2048]{1,0:T(8,128)(2,1)} %get-tuple-element.80) | copy-start | bytes 3145732
